TPU v7x, 512 devices: a whole 4x4x16 slice. The times are simulated.
512 devices in a mesh: dp: 4 (over x_hi, core), ctx: 128 (over y, z, x_lo).
Axes of the slice: x: 4 (x_hi: 2, x_lo: 2; x = x_hi * 2 + x_lo), y: 4, z: 16, core: 2. Of those that a mesh axis runs over, the one named last changes fastest.
Arguments:
- queries: bfloat16 [4, 16384, 704], P('dp', 'ctx'), may hold values from -6 to 6
- keys: bfloat16 [4, 16384, 704], P('dp', 'ctx'), may hold values from -6 to 6
- values: bfloat16 [4, 16384, 704], P('dp', 'ctx'), may hold values from -24 to 24
- patch_ids: int32 [4, 16384], P('dp'), may hold values from 0 to 511
- counts: int32 [4, 128], P('dp'), may hold values from 1 to 128, 8192 in all within a row
- cotangent: bfloat16 [4, 16384, 1408], P('dp', 'ctx'), may hold values from -6 to 6
- w_out: bfloat16 [704, 1408], P('dp'), may hold values from -0.21875 to 0.21875
Outputs:
- attended: bfloat16 [4, 16384, 1408], P('dp', 'ctx')
- grad_queries: bfloat16 [4, 16384, 704], P('dp', 'ctx')
- grad_keys: bfloat16 [4, 16384, 704], P('dp', 'ctx')
- grad_values: bfloat16 [4, 16384, 704], P('dp', 'ctx')
- grad_w_out: float32 [704, 1408], P('dp')
Inputs may be any that keep to these rules, and one draw needn't show every extreme that they name: patch_ids[r] is the kept patch's frame within its time shard times 256 plus its place in the frame; rows past a shard's count are padding. `counts`: each time shard's live rows come first in its 128 rows.
All inputs are finite; a program needn't handle non-finite values.
Results may differ from a plain program's by a relative error of at most 0.012.
The roundings to bfloat16 on the way count: a program that leaves them out, or rounds other values in their place, can miss the bound.
Values may be sent and summed in bfloat16 or wider, within the bound.
A program may use at most 64 MiB of HBM per device.

v0:
```python
from functools import partial

import jax
import jax.numpy as jnp
from jax import lax
from jax.sharding import PartitionSpec as P

HEAD = 88
HEADS = 8
PATCHES = 256
FR = 2
SPAN = 2
WIN = 4


masked_score = -1e30


def shifted(value, axis, steps):
    count = lax.axis_size(axis)
    first, last = (max(0, -steps), min(count, count - steps))
    return lax.ppermute(value, axis, [(source, source + steps) for source in range(first, last)])


def split_heads(matrix):
    return matrix.reshape(matrix.shape[0], HEADS, HEAD).transpose(1, 0, 2)


def join_heads(stacked):
    return stacked.transpose(1, 0, 2).reshape(stacked.shape[1], HEADS * HEAD)


def contract_last(left, right):
    return lax.dot_general(
        left, right, (((1,), (1,)), ((), ())), preferred_element_type=jnp.float32
    )


def contract_first(left, right):
    return lax.dot_general(
        left, right, (((0,), (0,)), ((), ())), preferred_element_type=jnp.float32
    )


def one_head(allowed, inputs):
    query_head, key_head, value_head, grad_head = inputs
    score_scale = HEAD ** (-0.5)
    scores = jnp.where(allowed, contract_last(query_head, key_head) * score_scale, masked_score)
    row_max = jnp.max(scores, axis=1, keepdims=True)
    expon = jnp.where(allowed, jnp.exp(scores - row_max), 0.0)
    row_sum = jnp.sum(expon, axis=1, keepdims=True)
    attention = (expon / row_sum).astype(jnp.bfloat16)
    context_head = jnp.dot(attention, value_head, preferred_element_type=jnp.float32).astype(
        jnp.bfloat16
    )
    row_delta = jnp.sum(
        grad_head.astype(jnp.float32) * context_head.astype(jnp.float32), axis=1, keepdims=True
    )
    grad_prob = contract_last(grad_head, value_head)
    grad_scores = (attention.astype(jnp.float32) * (grad_prob - row_delta)).astype(jnp.bfloat16)
    grad_query = (
        jnp.dot(grad_scores, key_head, preferred_element_type=jnp.float32) * score_scale
    ).astype(jnp.bfloat16)
    grad_key = contract_first(grad_scores, query_head) * score_scale
    grad_value = contract_first(attention, grad_head)
    return (
        context_head,
        grad_query,
        grad_key,
        grad_value,
        row_max[:, 0],
        row_sum[:, 0],
        row_delta[:, 0],
    )


def key_head(allowed, inputs):
    query_head, grad_head, key_part, value_part, row_max, row_sum, row_delta = inputs
    score_scale = HEAD ** (-0.5)
    scores = contract_last(query_head, key_part) * score_scale
    expon = jnp.where(
        allowed, jnp.exp(jnp.where(allowed, scores, masked_score) - row_max[:, None]), 0.0
    )
    attention = (expon / row_sum[:, None]).astype(jnp.bfloat16)
    grad_prob = contract_last(grad_head, value_part)
    grad_scores = (attention.astype(jnp.float32) * (grad_prob - row_delta[:, None])).astype(
        jnp.bfloat16
    )
    grad_key = contract_first(grad_scores, query_head) * score_scale
    grad_value = contract_first(attention, grad_head)
    return (grad_key, grad_value)


def per_device(queries, keys, values, patch_ids, counts, cotangent, w_out):
    query_rows = queries[0]
    key_rows = keys[0]
    value_rows = values[0]
    grad_out = cotangent[0]
    shard_rows = query_rows.shape[0]
    features = query_rows.shape[1]
    places = lax.axis_size("ctx")
    here = lax.axis_index("ctx")
    frames_all = (
        jnp.arange(places, dtype=jnp.int32)[:, None] * FR
        + patch_ids[0].reshape(places, shard_rows) // PATCHES
    )
    live_all = jnp.arange(shard_rows, dtype=jnp.int32)[None, :] < counts[0][:, None]

    def shard_of(offset):
        place = here + offset
        inside = (place >= 0) & (place < places)
        slot = jnp.clip(place, 0, places - 1)
        frames = lax.dynamic_index_in_dim(frames_all, slot, 0, keepdims=False)
        alive = lax.dynamic_index_in_dim(live_all, slot, 0, keepdims=False) & inside
        return (frames, alive, inside)

    own_frames, own_live, _ = shard_of(0)
    weights_full = lax.all_gather(w_out, "dp", axis=0, tiled=True)
    grad_live = jnp.where(own_live[:, None], grad_out, jnp.zeros_like(grad_out))
    grad_context = contract_last(grad_live, weights_full).astype(jnp.bfloat16)
    key_value = jnp.stack([key_rows, value_rows])
    offsets = list(range(-SPAN, SPAN + 1))
    fetched = []
    far_frames = []
    far_live = []
    for offset in offsets:
        if offset == 0:
            fetched.append(key_value)
        else:
            fetched.append(shifted(key_value, "ctx", -offset))
        frames, alive, _ = shard_of(offset)
        far_frames.append(frames)
        far_live.append(alive)
    window_keys = jnp.concatenate([piece[0] for piece in fetched], axis=0)
    window_values = jnp.concatenate([piece[1] for piece in fetched], axis=0)
    window_frames = jnp.concatenate(far_frames)
    window_live = jnp.concatenate(far_live)
    allowed = window_live[None, :] & (jnp.abs(own_frames[:, None] - window_frames[None, :]) <= WIN)
    results = lax.map(
        partial(one_head, allowed),
        (
            split_heads(query_rows),
            split_heads(window_keys),
            split_heads(window_values),
            split_heads(grad_context),
        ),
    )
    (
        context_heads,
        grad_query_heads,
        grad_key_heads,
        grad_value_heads,
        row_max,
        row_sum,
        row_delta,
    ) = results
    context = join_heads(context_heads)
    projected = jnp.dot(context, weights_full, preferred_element_type=jnp.float32)
    attended = jnp.where(own_live[:, None], projected, 0.0).astype(jnp.bfloat16)
    grad_queries = join_heads(grad_query_heads)
    key_terms = jnp.stack([join_heads(grad_key_heads), join_heads(grad_value_heads)]).reshape(
        2, len(offsets), shard_rows, features
    )
    summed = key_terms[:, SPAN]
    for position, offset in enumerate(offsets):
        if offset != 0:
            summed = summed + shifted(key_terms[:, position], "ctx", offset)
    grad_keys = summed[0].astype(jnp.bfloat16)
    grad_values = summed[1].astype(jnp.bfloat16)
    partial_weight = contract_first(context, grad_live)
    over_time = lax.psum(partial_weight, "ctx")
    grad_weight = lax.psum_scatter(over_time, "dp", scatter_dimension=0, tiled=True)
    return (attended[None], grad_queries[None], grad_keys[None], grad_values[None], grad_weight)


def solution(mesh):
    placed = (
        P("dp", "ctx", None),
        P("dp", "ctx", None),
        P("dp", "ctx", None),
        P("dp", None),
        P("dp", None),
        P("dp", "ctx", None),
        P("dp", None),
    )
    return jax.shard_map(
        per_device,
        mesh=mesh,
        in_specs=placed,
        out_specs=(
            P("dp", "ctx", None),
            P("dp", "ctx", None),
            P("dp", "ctx", None),
            P("dp", "ctx", None),
            P("dp", None),
        ),
        check_vma=False,
    )
```

profile of v0, /device:TPU:6, one launch (start us, length us, event | category | flops | bytes accessed | tf_op | source)
XLA Modules:
  0.0 1379.6 jit_solution(18419395530538153213)
XLA Ops:
  7.2 1.6 constant_dynamic-update-slice_fusion.1
  8.9 1.6 constant_dynamic-update-slice_fusion
  11.8 2.7 collective-permute-start.2
  14.5 4.0 collective-permute-start.1
  18.5 4.6 collective-permute-start
  26.1 8.1 collective-permute-done.1
  35.4 24.5 %all-gather.2.cloned.1.call-done = bf16[704,1408]{1,0:T(8,128)(2,1)} async-done(((bf16[176,1408]{1,0:T(8,128)(2,1)}), bf16[704,1408]{1,0:T(8,128)(2,1)}) %all-gather.2.cloned.1.call-update) | async-done | bytes 1982480 | tf_op jit(solution)/shard_map/all_gather | solution.py:118
  59.8 2.3 convolution_convert_fusion.1
  62.1 43.3 %while.17 = (s32[]{:T(128)}, bf16[8,128,88]{1,2,0:T(8,128)(2,1)S(1)}, bf16[8,128,88]{1,2,0:T(8,128)(2,1)}, f32[8,640,88]{1,2,0:T(8,128)}, f32[8,640,88]{1,2,0:T(...) while((s32[]{:T(128)}, ...), condition=%wide.region_4.5_spmd.clone, body=%wide.region_0.4_spmd.clone.sunk | while | flops 88772224 | bytes 3256713 | solution.py:139
  70.5 1.6 fusion.112
  81.3 1.6 fusion.112
  102.9 1.6 fusion.112
  105.4 2.7 fusion.42
  108.2 2.3 reshape.82
  110.5 3.1 reshape.81
  113.6 2.2 copy_dynamic-update-slice_fusion.1
  119.8 5.4 collective-permute-start.7
  125.2 2.0 collective-permute-start.6
  127.2 4.7 collective-permute-start.5
  131.9 55.5 %reduce-scatter.2.cloned.1.call-done = f32[176,1408]{1,0:T(8,128)} async-done(((f32[704,1408]{1,0:T(8,128)}), f32[176,1408]{1,0:T(8,128)}) %reduce-scatter.2.cloned.1.call-update) | async-done | bytes 991248 | tf_op jit(solution)/shard_map/reduce_scatter | solution.py:172
  187.5 2.2 fusion.36
  189.6 2.1 fusion.41
  192.5 1178.3 %all-reduce.2.cloned.1.call-done = f32[176,1408]{1,0:T(8,128)} async-done(((f32[176,1408]{1,0:T(8,128)}), f32[176,1408]{1,0:T(8,128)}) %all-reduce.2.cloned.1.call-update) | async-done | bytes 991248 | tf_op jit(solution)/shard_map/psum | solution.py:171
  1370.8 2.2 copy.96
  (133 shorter events, 48.2 us)
Async XLA Ops:
  7.2 27.3 %copy-start.3 = (bf16[1,128,704]{1,2,0:T(8,128)(2,1)S(1)}, bf16[1,128,704]{1,2,0:T(8,128)(2,1)}, u32[]{:S(2)}) copy-start(bf16[1,128,704]{1,2,0:T(8,128)(2,1)} %param.10) | copy-start | bytes 540676
  7.2 52.7 %all-gather.2.cloned.1.call-start = ((), (), s32[]{:S(2)}) async-start(), calls=%async_computation.1 | async-start | bytes 2478080 | tf_op jit(solution)/shard_map/all_gather | solution.py:118
  10.5 24.1 %collective-permute-start.3 = (bf16[2,128,704]{1,2,0:T(8,128)(2,1)}, bf16[2,128,704]{1,2,0:T(8,128)(2,1)S(1)}, u32[]{:S(2)}, u32[]{:S(2)}) collective-permute-start(bf16[2,128,704]{1,2,0:T(8,128)(2,1)} %constant_dynamic-update-slice_fusion), channel_id=1, source_target_pairs={{2,0},{3,1},{4,2},{5,3},{6,4},{7,5},{8,6},{9,7},{10,8},{11,9},{12,... | collective-permute-start | bytes 1081352 | tf_op jit(solution)/shard_map/ppermute | solution.py:22
  11.8 22.7 %collective-permute-start.2 = (bf16[2,128,704]{1,2,0:T(8,128)(2,1)}, bf16[2,128,704]{1,2,0:T(8,128)(2,1)S(1)}, u32[]{:S(2)}, u32[]{:S(2)}) collective-permute-start(bf16[2,128,704]{1,2,0:T(8,128)(2,1)} %constant_dynamic-update-slice_fusion), channel_id=1, source_target_pairs={{1,0},{2,1},{3,2},{4,3},{5,4},{6,5},{7,6},{8,7},{9,8},{10,9},{11,1... | collective-permute-start | bytes 1081352 | tf_op jit(solution)/shard_map/ppermute | solution.py:22
  14.5 19.7 %collective-permute-start.1 = (bf16[2,128,704]{1,2,0:T(8,128)(2,1)}, bf16[2,128,704]{1,2,0:T(8,128)(2,1)S(1)}, u32[]{:S(2)}, u32[]{:S(2)}) collective-permute-start(bf16[2,128,704]{1,2,0:T(8,128)(2,1)} %constant_dynamic-update-slice_fusion), channel_id=1, source_target_pairs={{0,1},{1,2},{2,3},{3,4},{4,5},{5,6},{6,7},{7,8},{8,9},{9,10},{10,1... | collective-permute-start | bytes 1081352 | tf_op jit(solution)/shard_map/ppermute | solution.py:22
  18.5 15.7 %collective-permute-start = (bf16[2,128,704]{1,2,0:T(8,128)(2,1)}, bf16[2,128,704]{1,2,0:T(8,128)(2,1)S(1)}, u32[]{:S(2)}, u32[]{:S(2)}) collective-permute-start(bf16[2,128,704]{1,2,0:T(8,128)(2,1)} %constant_dynamic-update-slice_fusion), channel_id=1, source_target_pairs={{0,2},{1,3},{2,4},{3,5},{4,6},{5,7},{6,8},{7,9},{8,10},{9,11},{10,... | collective-permute-start | bytes 1081352 | tf_op jit(solution)/shard_map/ppermute | solution.py:22
  23.1 164.3 %reduce-scatter.2.cloned.1.call-start = ((), (), s32[]{:S(2)}) async-start(), calls=%async_computation.2 | async-start | bytes 4956160 | tf_op jit(solution)/shard_map/reduce_scatter | solution.py:172
  34.3 0.9 copy-start.4
  34.4 25.4 %copy-start.2 = (bf16[1,128,1408]{2,1,0:T(8,128)(2,1)S(1)}, bf16[1,128,1408]{2,1,0:T(8,128)(2,1)}, u32[]{:S(2)}) copy-start(bf16[1,128,1408]{2,1,0:T(8,128)(2,1)} %param.14) | copy-start | bytes 1081348
  105.4 2.7 copy-start.5
  108.2 1262.6 %all-reduce.2.cloned.1.call-start = ((), (), s32[]{:S(2)}) async-start(), calls=%async_computation.3 | async-start | bytes 1982464 | tf_op jit(solution)/shard_map/psum | solution.py:171
  116.1 2.4 copy-start
  116.1 71.4 %copy-start.1 = (bf16[704,1408]{1,0:T(8,128)(2,1)S(1)}, bf16[704,1408]{1,0:T(8,128)(2,1)}, u32[]{:S(2)}) copy-start(bf16[704,1408]{1,0:T(8,128)(2,1)} %all-gather.2.cloned.1.call-done) | copy-start | bytes 5947396
  118.5 71.2 %collective-permute-start.4 = (f32[2,128,704]{1,2,0:T(8,128)}, f32[2,128,704]{1,2,0:T(8,128)}, u32[]{:S(2)}, u32[]{:S(2)}) collective-permute-start(f32[2,128,704]{1,2,0:T(8,128)} %get-tuple-element.169), channel_id=1, source_target_pairs={{2,0},{3,1},{4,2},{5,3},{6,4},{7,5},{8,6},{9,7},{10,8},{11,9},{12,... | collective-permute-start | bytes 2162696 | tf_op jit(solution)/shard_map/ppermute | solution.py:22
  119.8 69.9 %collective-permute-start.7 = (f32[2,128,704]{1,2,0:T(8,128)}, f32[2,128,704]{1,2,0:T(8,128)}, u32[]{:S(2)}, u32[]{:S(2)}) collective-permute-start(f32[2,128,704]{1,2,0:T(8,128)} %get-tuple-element.170), channel_id=1, source_target_pairs={{0,2},{1,3},{2,4},{3,5},{4,6},{5,7},{6,8},{7,9},{8,10},{9,11},{10,... | collective-permute-start | bytes 2162696 | tf_op jit(solution)/shard_map/ppermute | solution.py:22
  125.2 64.4 %collective-permute-start.6 = (f32[2,128,704]{1,2,0:T(8,128)S(1)}, f32[2,128,704]{1,2,0:T(8,128)}, u32[]{:S(2)}, u32[]{:S(2)}) collective-permute-start(f32[2,128,704]{1,2,0:T(8,128)S(1)} %get-tuple-element.171), channel_id=1, source_target_pairs={{0,1},{1,2},{2,3},{3,4},{4,5},{5,6},{6,7},{7,8},{8,9},{9,10},{10,1... | collective-permute-start | bytes 2162696 | tf_op jit(solution)/shard_map/ppermute | solution.py:22
  127.2 62.5 %collective-permute-start.5 = (f32[2,128,704]{1,2,0:T(8,128)S(1)}, f32[2,128,704]{1,2,0:T(8,128)}, u32[]{:S(2)}, u32[]{:S(2)}) collective-permute-start(f32[2,128,704]{1,2,0:T(8,128)S(1)} %get-tuple-element.172), channel_id=1, source_target_pairs={{1,0},{2,1},{3,2},{4,3},{5,4},{6,5},{7,6},{8,7},{9,8},{10,9},{11,1... | collective-permute-start | bytes 2162696 | tf_op jit(solution)/shard_map/ppermute | solution.py:22
Sparse Core Ops, SparseCore 0:
  23.2 36.5 all-gather.1
  108.3 79.0 reduce-scatter.1
  190.6 1180.1 all-reduce.1
where the time goes:
time: 1380 us
  waiting for transfers between devices  1270 us (92%)
  matrix products  45.7 us (3%)
  starting transfers between devices  26.1 us (2%)
  local copies, waits for them, and re-layouts  18.5 us (1%)
  between operations  14.2 us (1%)
    psum x1, waiting for transfers between devices, per_device(): over_time = lax.psum(partial_weight, 'ctx')  1180 us
    reduce_scatter x1, waiting for transfers between devices, per_device(): lax.psum_scatter(over_time, 'dp', scatter_dimension=0, tiled=True)  55.5 us
  transfers between devices with their start and end apart: 11, of which 4 were waited for; matrix products, arithmetic and copies ran while one was open for 1% of the time, Pallas kernels for 0%

commit v1 on v0

v1 whole, which is shorter than its diff:
```python
import jax
import jax.numpy as jnp
from jax import lax
from jax.experimental import pallas as pl
from jax.experimental.pallas import tpu as pltpu
from jax.sharding import PartitionSpec as P

HEAD = 88
WIN = 4
ROWS = 128
HALF = 352
WIDE = 384
HW = 704
D = 1408
BLOCK = 176
SLOTS = 6
PLACES = 128
SCALE = HEAD ** -0.5
MASKED = -1e30
TILES = 121
MESH = pl.DeviceIdType.MESH
WINDOWS = ((0, 128), (0, 256), (128, 384), (256, 384))
BF = jnp.bfloat16
F32 = jnp.float32


def last_last(left, right):
    return lax.dot_general(left, right, (((1,), (1,)), ((), ())), preferred_element_type=F32)


def first_first(left, right):
    return lax.dot_general(left, right, (((0,), (0,)), ((), ())), preferred_element_type=F32)


def plain(left, right):
    return jnp.dot(left, right, preferred_element_type=F32)


def head_mask(head, rows):
    low, high = WINDOWS[head]
    lane = lax.broadcasted_iota(jnp.int32, (rows, high - low), 1) + low
    return jnp.where((lane >= HEAD * head) & (lane < HEAD * (head + 1)), 1.0, 0.0)


def kernel(q_ref, k_ref, v_ref, pid_ref, cnt_ref, cot_ref, w_ref,
           att_ref, gq_ref, gk_ref, gv_ref, gw_ref,
           kh, vh, qh, kw, vw, qw, gl, wf, bias, s_buf, probs, ds_buf,
           ctx_acc, cw, cf, ctb, ct, g_buf, dq_acc, dk_acc, dv_acc, dqw, dqf,
           dkb, dvb, rk, rv, dks, dvs, dkf, dvf,
           dw, ry, sx, rx, sz, rz, gf,
           k_rs, v_rs, q_rs, gl_rs, w_rs, c_rs, dq_rs, dk_rs, dv_rs, y_rs, x_rs, z_rs,
           ss, x_ss, z_ss):
    dp = lax.axis_index("dp")
    place = lax.axis_index("ctx")
    xh = lax.div(dp, 2)
    core = lax.rem(dp, 2)
    pair = lax.div(place, 2)
    xl = lax.rem(place, 2)
    y = lax.div(place, 32)
    z = lax.rem(pair, 16)
    spot = y * 2 + xl

    partner = (dp, place + 1 - 2 * xl)
    twin = (dp + 1 - 2 * core, place)
    other = lax.rem(dp + 2, 4)
    across = (other, place + 1 - 2 * xl)
    ahead = (dp, lax.rem(place + 2, PLACES))
    behind = (dp, lax.rem(place + PLACES - 2, PLACES))

    def around(j):
        where = lax.rem(spot + j, 8)
        return (dp, lax.div(where, 2) * 32 + z * 2 + lax.rem(where, 2))

    def along(j):
        return (dp, (y * 16 + lax.rem(z + j, 16)) * 2 + xl)

    barrier = pltpu.get_barrier_semaphore()
    for device in (twin, partner, across, (other, place), ahead, behind):
        pl.semaphore_signal(barrier, inc=1, device_id=device, device_id_type=MESH)

    def greet_around(j, carry):
        pl.semaphore_signal(barrier, inc=1, device_id=around(j), device_id_type=MESH)
        return carry

    def greet_along(j, carry):
        pl.semaphore_signal(barrier, inc=1, device_id=along(j), device_id_type=MESH)
        return carry

    lax.fori_loop(1, 8, greet_around, 0)
    lax.fori_loop(1, 16, greet_along, 0)

    pad = jnp.zeros((ROWS, 128), BF)
    for source, halves in ((k_ref, kh), (v_ref, vh), (q_ref, qh)):
        for half in range(2):
            halves[half, :, 256:384] = pad
            halves[half, :, 0:HALF] = source[:, half * HALF:(half + 1) * HALF]
    kw[2 + xl] = kh[xl]
    vw[2 + xl] = vh[xl]
    qw[xl] = qh[xl]

    own_live = lax.broadcasted_iota(jnp.int32, (ROWS, 128), 0) < cnt_ref[0, place]
    mine = core * 2 + xl
    for block in range(11):
        cols = slice(block * 128, (block + 1) * 128)
        gl[mine, :, cols] = jnp.where(own_live, cot_ref[:, cols].astype(F32), 0.0).astype(BF)

    pl.semaphore_wait(barrier, 28)

    sent = []

    def send(source, target, recv_sem, device):
        copy = pltpu.make_async_remote_copy(
            src_ref=source, dst_ref=target, send_sem=ss.at[len(sent)], recv_sem=recv_sem,
            device_id=device, device_id_type=MESH)
        copy.start()
        sent.append(copy)

    def arrived(ref, recv_sem):
        pltpu.make_async_remote_copy(
            src_ref=ref, dst_ref=ref, send_sem=ss.at[0], recv_sem=recv_sem,
            device_id=partner, device_id_type=MESH).wait_recv()

    far = 3 - xl
    send(kh.at[1 - xl], kw.at[2 + xl], k_rs.at[2 + xl], partner)
    send(kh.at[xl], kw.at[xl], k_rs.at[xl], ahead)
    send(kh.at[xl], kw.at[4 + xl], k_rs.at[4 + xl], behind)
    send(qh.at[1 - xl], qw.at[xl], q_rs, partner)
    send(vh.at[1 - xl], vw.at[2 + xl], v_rs.at[2 + xl], partner)
    send(w_ref, wf.at[dp], w_rs.at[dp], across)
    send(w_ref, wf.at[dp], w_rs.at[dp], twin)
    send(gl.at[mine], gl.at[mine], gl_rs.at[mine], twin)
    wf[dp] = w_ref[...]

    key_frames = []
    for slot in range(SLOTS):
        shard = lax.rem(2 * pair - 2 + slot + PLACES, PLACES)
        inside = (2 * pair - 2 + slot >= 0) & (2 * pair - 2 + slot < PLACES)
        count = jnp.where(inside, cnt_ref[0, shard], 0)
        frame = lax.shift_right_logical(pid_ref[pl.ds(shard, 1), :], 8) + 2 * (slot - 2)
        key_frames.append((frame, count))
    for slot, (frame, count) in enumerate(key_frames):
        column = jnp.transpose(jnp.broadcast_to(frame.astype(F32), (ROWS, 128)))
        alive = lax.broadcasted_iota(jnp.int32, (ROWS, 128), 0) < count
        for half in range(2):
            row = key_frames[2 + half][0].astype(F32)
            seen = alive & (jnp.abs(row - column) <= WIN)
            bias[slot, :, half * 128:(half + 1) * 128] = jnp.where(seen, 0.0, MASKED)

    arrived(kw.at[far], k_rs.at[far])
    send(kw.at[far], kw.at[1 - xl], k_rs.at[1 - xl], ahead)
    send(kw.at[far], kw.at[5 - xl], k_rs.at[5 - xl], behind)
    send(vh.at[xl], vw.at[xl], v_rs.at[xl], ahead)
    send(vh.at[xl], vw.at[4 + xl], v_rs.at[4 + xl], behind)
    arrived(qw.at[1 - xl], q_rs)
    arrived(vw.at[far], v_rs.at[far])
    send(vw.at[far], vw.at[1 - xl], v_rs.at[1 - xl], ahead)
    send(vw.at[far], vw.at[5 - xl], v_rs.at[5 - xl], behind)
    send(gl.at[mine], gl.at[mine], gl_rs.at[mine], partner)
    for slot in (0, 1, 4, 5):
        arrived(kw.at[slot], k_rs.at[slot])

    def add_to(ref, head, value, seen):
        low, high = WINDOWS[head]
        for start in range(low, high, 128):
            part = value[:, start - low:start - low + 128]
            if start in seen:
                ref[:, start:start + 128] += part
            else:
                ref[:, start:start + 128] = part
                seen.add(start)

    seen = set()
    for head in range(4):
        low, high = WINDOWS[head]
        q_head = qw[:, :, low:high].reshape(256, high - low) * head_mask(head, 256).astype(BF)
        top = None
        for slot in range(SLOTS):
            score = last_last(kw[slot, :, low:high], q_head) * SCALE + bias[slot]
            s_buf[slot] = score
            high_here = jnp.max(score, axis=0, keepdims=True)
            top = high_here if top is None else jnp.maximum(top, high_here)
        total = None
        for slot in range(SLOTS):
            expon = jnp.exp(s_buf[slot] - top)
            s_buf[slot] = expon
            here = jnp.sum(expon, axis=0, keepdims=True)
            total = here if total is None else total + here
        inverse = 1.0 / total
        for slot in range(SLOTS):
            probs[head, slot] = (s_buf[slot] * inverse).astype(BF)
        if head == 0:
            for slot in (0, 1, 4, 5):
                arrived(vw.at[slot], v_rs.at[slot])
        part = first_first(probs[head].reshape(768, 256), vw[:, :, low:high].reshape(768, high - low))
        add_to(ctx_acc, head, part * head_mask(head, 256), seen)
    context = ctx_acc[...].astype(BF)
    ctb[0] = context[:, 0:BLOCK]
    ctb[1] = context[:, BLOCK:HALF]
    send(ctb.at[1 - core], ct.at[core], c_rs.at[0], twin)
    cw[...] = context.reshape(2, ROWS, WIDE)
    send(cw.at[1 - xl], cf.at[xl], c_rs.at[1], partner)
    ct[core] = ctb[core]
    cf[xl] = cw[xl]

    arrived(wf.at[other], w_rs.at[other])
    send(wf.at[other], wf.at[other], w_rs.at[other], twin)
    theirs = core * 2 + 1 - xl
    arrived(gl.at[theirs], gl_rs.at[theirs])
    send(gl.at[theirs], gl.at[theirs], gl_rs.at[theirs], twin)
    arrived(wf.at[dp + 1 - 2 * core], w_rs.at[dp + 1 - 2 * core])
    arrived(wf.at[other + 1 - 2 * core], w_rs.at[other + 1 - 2 * core])
    grad_context = last_last(gl[pl.ds(core * 2, 2)].reshape(256, D), wf[pl.ds(xl * 2, 2)].reshape(HALF, D))
    g_buf[:, 256:384] = jnp.zeros((256, 128), BF)
    g_buf[:, 0:HALF] = grad_context.astype(BF)

    arrived(ct.at[1 - core], c_rs.at[0])
    for slot in range(2):
        there = (1 - core) * 2 + slot
        arrived(gl.at[there], gl_rs.at[there])
    turned = jnp.transpose(ct[...].reshape(512, BLOCK).astype(F32)).astype(BF)
    for start in range(0, D, 256):
        stop = min(start + 256, D)
        part = plain(turned, gl[:, :, start:stop].reshape(512, stop - start))
        for column in range(start, stop, 128):
            for row in range(11):
                tile = row * 11 + column // 128
                dw[tile // 32, tile % 32] = part[row * 16:row * 16 + 16, column - start:column - start + 128].astype(BF)
    for tile in range(TILES, 128):
        dw[tile // 32, tile % 32] = jnp.zeros((16, 128), BF)
    for step in (1, 3, 2):
        goal = lax.rem(y + step, 4)
        send(dw.at[goal], ry.at[step - 1], y_rs.at[step - 1], (dp, lax.rem(place + 32 * step, PLACES)))

    seen_q, seen_k, seen_v = set(), set(), set()
    for head in range(4):
        low, high = WINDOWS[head]
        mask = head_mask(head, 256)
        q_head = qw[:, :, low:high].reshape(256, high - low) * mask.astype(BF)
        g_head = g_buf[:, low:high] * mask.astype(BF)
        delta = None
        for slot in range(SLOTS):
            grad_prob = last_last(vw[slot, :, low:high], g_head)
            s_buf[slot] = grad_prob
            here = jnp.sum(probs[head, slot].astype(F32) * grad_prob, axis=0, keepdims=True)
            delta = here if delta is None else delta + here
        for slot in range(SLOTS):
            ds_buf[slot] = (probs[head, slot].astype(F32) * (s_buf[slot] - delta)).astype(BF)
        grad_scores = ds_buf[...].reshape(768, 256)
        part = first_first(grad_scores, kw[:, :, low:high].reshape(768, high - low))
        add_to(dq_acc, head, part * mask, seen_q)
        add_to(dk_acc, head, plain(grad_scores, q_head), seen_k)
        add_to(dv_acc, head, plain(probs[head].reshape(768, 256), g_head), seen_v)
    dkb[...] = (dk_acc[...] * SCALE).astype(BF).reshape(SLOTS, ROWS, WIDE)
    send(dkb.at[pl.ds(0, 2)], rk.at[1], dk_rs.at[1], behind)
    send(dkb.at[pl.ds(4, 2)], rk.at[0], dk_rs.at[0], ahead)
    dvb[...] = dv_acc[...].astype(BF).reshape(SLOTS, ROWS, WIDE)
    send(dvb.at[pl.ds(0, 2)], rv.at[1], dv_rs.at[1], behind)
    send(dvb.at[pl.ds(4, 2)], rv.at[0], dv_rs.at[0], ahead)
    dqw[...] = (dq_acc[...] * SCALE).astype(BF).reshape(2, ROWS, WIDE)
    send(dqw.at[1 - xl], dqf.at[xl], dq_rs, partner)
    dqf[xl] = dqw[xl]

    for step in range(3):
        arrived(ry.at[step], y_rs.at[step])
    total = dw[y].astype(F32) + ry[0].astype(F32) + ry[1].astype(F32) + ry[2].astype(F32)
    sx[...] = total.astype(BF).reshape(2, 16, 16, 128)

    def x_copy(half):
        return pltpu.make_async_remote_copy(
            src_ref=sx.at[half], dst_ref=rx.at[xh], send_sem=x_ss.at[half], recv_sem=x_rs.at[xh],
            device_id=(2 * xl + core, 2 * pair + half), device_id_type=MESH)

    for half in range(2):
        stays = (xh == xl) & (xl == half)

        @pl.when(stays)
        def _():
            rx[xh] = sx[half]

        @pl.when(jnp.logical_not(stays))
        def _():
            x_copy(half).start()

    arrived(cf.at[1 - xl], c_rs.at[1])
    projected = plain(cf[0][:, 0:HALF], wf[pl.ds(0, 2)].reshape(HALF, D))
    projected = projected + plain(cf[1][:, 0:HALF], wf[pl.ds(2, 2)].reshape(HALF, D))
    for block in range(11):
        cols = slice(block * 128, (block + 1) * 128)
        att_ref[:, cols] = jnp.where(own_live, projected[:, cols], 0.0).astype(BF)

    for source in range(2):
        @pl.when(jnp.logical_not((xh == xl) & (xh == source)))
        def _():
            arrived(rx.at[source], x_rs.at[source])

    sz[...] = (rx[0].astype(F32) + rx[1].astype(F32)).astype(BF)

    def scatter(j, carry):
        pltpu.make_async_remote_copy(
            src_ref=sz.at[lax.rem(z + j, 16)], dst_ref=rz.at[j - 1], send_sem=z_ss.at[0], recv_sem=z_rs.at[0],
            device_id=along(j), device_id_type=MESH).start()
        return carry

    lax.fori_loop(1, 16, scatter, 0)

    def gather_grad(terms, near, near_sems, summed, full, acc, scale, sem):
        arrived(near.at[0], near_sems.at[0])
        arrived(near.at[1], near_sems.at[1])
        value = acc[256:512, :].reshape(2, ROWS, WIDE) * scale + near[0].astype(F32) + near[1].astype(F32)
        summed[...] = value.astype(BF)
        send(summed.at[1 - xl], full.at[xl], sem, partner)
        full[xl] = summed[xl]

    def many(sem, ref, send_sem):
        return pltpu.make_async_remote_copy(
            src_ref=ref, dst_ref=ref, send_sem=send_sem, recv_sem=sem, device_id=partner, device_id_type=MESH)

    many(z_rs.at[0], rz, z_ss.at[0]).wait_recv()
    total = sz[z].astype(F32)
    for step in range(15):
        total = total + rz[step].astype(F32)
    gf[spot, z] = total.astype(BF)

    def spread(j, carry):
        pltpu.make_async_remote_copy(
            src_ref=gf.at[spot, z], dst_ref=gf.at[spot, z], send_sem=z_ss.at[1], recv_sem=z_rs.at[1],
            device_id=along(j), device_id_type=MESH).start()
        return carry

    lax.fori_loop(1, 16, spread, 0)

    gather_grad(dkb, rk, dk_rs, dks, dkf, dk_acc, SCALE, dk_rs.at[2])
    gather_grad(dvb, rv, dv_rs, dvs, dvf, dv_acc, 1.0, dv_rs.at[2])

    many(z_rs.at[1], rz, z_ss.at[1]).wait_recv()

    def share(j, carry):
        pltpu.make_async_remote_copy(
            src_ref=gf.at[spot], dst_ref=gf.at[spot], send_sem=z_ss.at[2], recv_sem=z_rs.at[2],
            device_id=around(j), device_id_type=MESH).start()
        return carry

    lax.fori_loop(1, 8, share, 0)

    for full, sem, out in ((dqf, dq_rs, gq_ref), (dkf, dk_rs.at[2], gk_ref), (dvf, dv_rs.at[2], gv_ref)):
        arrived(full.at[1 - xl], sem)
        for half in range(2):
            out[:, half * HALF:(half + 1) * HALF] = full[half, :, 0:HALF]

    many(z_rs.at[2], gf.at[pl.ds(0, 7)], z_ss.at[2]).wait_recv()
    for tile in range(TILES):
        row, column = tile // 11, tile % 11
        gw_ref[row * 16:row * 16 + 16, column * 128:(column + 1) * 128] = gf[tile // 16, tile % 16].astype(F32)

    for copy in sent:
        copy.wait_send()
    for half in range(2):
        @pl.when(jnp.logical_not((xh == xl) & (xl == half)))
        def _():
            x_copy(half).wait_send()
    many(z_rs.at[0], rz, z_ss.at[0]).wait_send()
    many(z_rs.at[1], rz, z_ss.at[1]).wait_send()
    many(z_rs.at[2], gf.at[pl.ds(0, 7)], z_ss.at[2]).wait_send()


def per_device(queries, keys, values, patch_ids, counts, cotangent, w_out):
    vmem = pl.BlockSpec(memory_space=pltpu.VMEM)
    smem = pl.BlockSpec(memory_space=pltpu.SMEM)
    pair_rows = (2, ROWS, WIDE)
    window = (SLOTS, ROWS, WIDE)
    dma = pltpu.SemaphoreType.DMA
    scratch = [
        pltpu.VMEM(pair_rows, BF), pltpu.VMEM(pair_rows, BF), pltpu.VMEM(pair_rows, BF),
        pltpu.VMEM(window, BF), pltpu.VMEM(window, BF), pltpu.VMEM(pair_rows, BF),
        pltpu.VMEM((4, ROWS, D), BF), pltpu.VMEM((4, BLOCK, D), BF),
        pltpu.VMEM((SLOTS, ROWS, 256), F32), pltpu.VMEM((SLOTS, ROWS, 256), F32),
        pltpu.VMEM((4, SLOTS, ROWS, 256), BF), pltpu.VMEM((SLOTS, ROWS, 256), BF),
        pltpu.VMEM((256, WIDE), F32), pltpu.VMEM(pair_rows, BF), pltpu.VMEM(pair_rows, BF),
        pltpu.VMEM((2, 256, BLOCK), BF), pltpu.VMEM((2, 256, BLOCK), BF), pltpu.VMEM((256, WIDE), BF),
        pltpu.VMEM((256, WIDE), F32), pltpu.VMEM((768, WIDE), F32), pltpu.VMEM((768, WIDE), F32),
        pltpu.VMEM(pair_rows, BF), pltpu.VMEM(pair_rows, BF),
        pltpu.VMEM(window, BF), pltpu.VMEM(window, BF),
        pltpu.VMEM((2,) + pair_rows, BF), pltpu.VMEM((2,) + pair_rows, BF),
        pltpu.VMEM(pair_rows, BF), pltpu.VMEM(pair_rows, BF), pltpu.VMEM(pair_rows, BF), pltpu.VMEM(pair_rows, BF),
        pltpu.VMEM((4, 32, 16, 128), BF), pltpu.VMEM((3, 32, 16, 128), BF),
        pltpu.VMEM((2, 16, 16, 128), BF), pltpu.VMEM((2, 16, 16, 128), BF),
        pltpu.VMEM((16, 16, 128), BF), pltpu.VMEM((15, 16, 128), BF), pltpu.VMEM((8, 16, 16, 128), BF),
        dma((6,)), dma((6,)), dma, dma((4,)), dma((4,)), dma((2,)), dma, dma((3,)), dma((3,)), dma((3,)),
        dma((2,)), dma((3,)),
        dma((32,)), dma((2,)), dma((3,)),
    ]
    outs = pl.pallas_call(
        kernel,
        out_shape=(
            jax.ShapeDtypeStruct((ROWS, D), BF),
            jax.ShapeDtypeStruct((ROWS, HW), BF),
            jax.ShapeDtypeStruct((ROWS, HW), BF),
            jax.ShapeDtypeStruct((ROWS, HW), BF),
            jax.ShapeDtypeStruct((BLOCK, D), F32),
        ),
        in_specs=[vmem, vmem, vmem, vmem, smem, vmem, vmem],
        out_specs=(vmem,) * 5,
        scratch_shapes=scratch,
        compiler_params=pltpu.CompilerParams(
            collective_id=0, has_side_effects=True, vmem_limit_bytes=48 * 1024 * 1024),
        cost_estimate=pl.CostEstimate(flops=1500000000, bytes_accessed=4000000, transcendentals=800000),
    )(queries[0], keys[0], values[0], patch_ids.reshape(PLACES, ROWS), counts, cotangent[0], w_out)
    attended, grad_queries, grad_keys, grad_values, grad_weight = outs
    return attended[None], grad_queries[None], grad_keys[None], grad_values[None], grad_weight


def solution(mesh):
    placed = (
        P("dp", "ctx", None),
        P("dp", "ctx", None),
        P("dp", "ctx", None),
        P("dp", None),
        P("dp", None),
        P("dp", "ctx", None),
        P("dp", None),
    )
    return jax.shard_map(
        per_device,
        mesh=mesh,
        in_specs=placed,
        out_specs=(
            P("dp", "ctx", None),
            P("dp", "ctx", None),
            P("dp", "ctx", None),
            P("dp", "ctx", None),
            P("dp", None),
        ),
        check_vma=False,
    )
```

time: 1380 us -> 87.2 us (0.06)
  waiting for transfers between devices: 1270 us -> 0 us
  Pallas kernels: 0 us -> 77.9 us
  matrix products: 45.7 us -> 0 us
  starting transfers between devices: 26.1 us -> 0 us
    psum x1 -> x0, waiting for transfers between devices: 1180 us -> none  [per_device(): over_time = lax.psum(partial_weight, 'ctx')]
    pallas_call x0 -> x1, Pallas kernels: none -> 77.9 us  [per_device(): pl.pallas_call(kernel, out_shape=(jax.ShapeDtypeStruct((ROWS, D), BF), ja...]
    reduce_scatter x1 -> x0, waiting for transfers between devices: 55.5 us -> none  [per_device(): lax.psum_scatter(over_time, 'dp', scatter_dimension=0, tiled=True)]
    dot_general x51 -> x0, matrix products: 45.7 us -> none  [the longest x17 22.5 us: contract_first(): lax.dot_general(left, right, (((0,), (0,)), ((), ())), preferred_element_...]
    ppermute x8 -> x0, starting transfers between devices: 26 us -> none  [shifted(): lax.ppermute(value, axis, [(source, source + steps) for source in range(f...]
    all_gather x1 -> x0, waiting for transfers between devices: 24.5 us -> none  [per_device(): weights_full = lax.all_gather(w_out, 'dp', axis=0, tiled=True)]
  transfers between devices with their start and end apart: 11 -> 0, of which waited for: 4 -> 0; matrix products, arithmetic and copies ran while one was open for 1% -> 0% of each run, Pallas kernels for 0% -> 0%
where the time goes in v1:
time: 87.2 us; the launch traced here: 85.7 us
  Pallas kernels  77.9 us (89%)
  local copies, waits for them, and re-layouts  7.1 us (8%)
    pallas_call x1, Pallas kernels, per_device(): pl.pallas_call(kernel, out_shape=(jax.ShapeDtypeStruct((ROWS, D), BF), ja...  77.9 us
    unnamed x18, local copies, waits for them, and re-layouts  7.1 us

profile of v1, /device:TPU:6, one launch (start us, length us, event | category | flops | bytes accessed | tf_op | source)
XLA Modules:
  0.0 85.7 jit_solution(16936469890550444667)
XLA Ops:
  0.6 0.0 copy-start.4
  0.6 0.0 copy-start
  0.7 1.1 %copy.12 = bf16[1,128,704]{2,1,0:T(8,128)(2,1)S(1)} copy(bf16[1,128,704]{1,2,0:T(8,128)(2,1)} %param.7) | data formatting | bytes 360448 | tf_op args[0]
  1.8 0.0 copy-done.4
  1.8 0.0 copy-start.1
  1.8 0.1 copy.13
  2.0 0.0 copy-start.2
  2.0 1.1 %copy.14 = bf16[1,128,704]{2,1,0:T(8,128)(2,1)S(1)} copy(bf16[1,128,704]{1,2,0:T(8,128)(2,1)} %param.9) | data formatting | bytes 360448 | tf_op args[2]
  3.1 0.0 copy-start.3
  3.1 0.0 copy-done
  3.1 0.0 copy-done.1
  3.1 0.0 copy-done.2
  3.1 0.6 copy-done.3
  3.7 77.9 %shard_map.110 = (bf16[128,1408]{1,0:T(8,128)(2,1)S(1)}, bf16[128,704]{1,0:T(8,128)(2,1)S(1)}, bf16[128,704]{1,0:T(8,128)(2,1)S(1)}, bf16[128,704]{1,0:T(8,128)(2,1)S(1)}, f32[176,1408]{1,0:T(8,128)S(1)}) custom-call(bf16[128,704]{1,0:T(8,128)(2,1)S(1)} %bitcast.13, bf16[128,704]{1,0:T(8,128)(2,1)S(1)} %bitcast.14, bf16[128,704]{1,0:T(8,128)(2,1)S(1)} %bitcast.15, ...), custom_call_target="tpu_custom_call" | custom-call | flops 1500000000 | bytes 4000000 | tf_op jit(solution)/shard_map/pallas_call | solution.py:392
  81.6 0.8 copy.15
  82.4 0.8 copy.16
  83.2 0.8 copy.17
  84.0 0.7 copy.20
  84.8 0.9 %copy.21 = f32[176,1408]{1,0:T(8,128)} copy(f32[176,1408]{1,0:T(8,128)S(1)} %get-tuple-element.29) | data formatting | bytes 1982464
Async XLA Ops:
  0.6 1.1 %copy-start.4 = (bf16[1,128,704]{1,2,0:T(8,128)(2,1)S(1)}, bf16[1,128,704]{1,2,0:T(8,128)(2,1)}, u32[]{:S(2)}) copy-start(bf16[1,128,704]{1,2,0:T(8,128)(2,1)} %param.8) | copy-start | bytes 540676
  0.6 2.4 %copy-start = (bf16[176,1408]{1,0:T(8,128)(2,1)S(1)}, bf16[176,1408]{1,0:T(8,128)(2,1)}, u32[]{:S(2)}) copy-start(bf16[176,1408]{1,0:T(8,128)(2,1)} %w_ref.1) | copy-start | bytes 1486852
  1.8 1.3 %copy-start.1 = (bf16[1,128,1408]{2,1,0:T(8,128)(2,1)S(1)}, bf16[1,128,1408]{2,1,0:T(8,128)(2,1)}, u32[]{:S(2)}) copy-start(bf16[1,128,1408]{2,1,0:T(8,128)(2,1)} %param.12) | copy-start | bytes 1081348
  2.0 1.1 %copy-start.2 = (s32[1,16384]{1,0:T(1,128)S(1)}, s32[1,16384]{1,0:T(1,128)}, u32[]{:S(2)}) copy-start(s32[1,16384]{1,0:T(1,128)} %param.10) | copy-start | bytes 196612
  3.1 0.7 copy-start.3

commit v2 on v1

v2 whole, which is shorter than its diff:
```python
import jax
import jax.numpy as jnp
from jax import lax
from jax.experimental import pallas as pl
from jax.experimental.pallas import tpu as pltpu
from jax.sharding import PartitionSpec as P

HEAD = 88
WIN = 4
ROWS = 128
HALF = 352
HW = 704
D = 1408
BLOCK = 176
SLOTS = 6
PLACES = 128
SCALE = HEAD ** -0.5
MASKED = -1e30
TILES = 121
MESH = pl.DeviceIdType.MESH
WINDOWS = ((0, 128), (0, 256), (128, 352), (256, 352))
STRIPES = ((0, 96), (80, 176), (176, 272), (256, 352))
BF = jnp.bfloat16
F32 = jnp.float32


def last_last(left, right):
    return lax.dot_general(left, right, (((1,), (1,)), ((), ())), preferred_element_type=F32)


def first_first(left, right):
    return lax.dot_general(left, right, (((0,), (0,)), ((), ())), preferred_element_type=F32)


def plain(left, right):
    return jnp.dot(left, right, preferred_element_type=F32)


def head_mask(head, rows):
    low, high = WINDOWS[head]
    lane = lax.broadcasted_iota(jnp.int32, (rows, high - low), 1) + low
    return jnp.where((lane >= HEAD * head) & (lane < HEAD * (head + 1)), 1.0, 0.0)


def stripe(head, value):
    skip = HEAD * head - STRIPES[head][0]
    return value[skip:skip + HEAD]


def kernel(q_ref, k_ref, v_ref, pid_ref, cnt_ref, cot_ref, w_ref,
           att_ref, gq_ref, gk_ref, gv_ref, gw_ref,
           kw, vw, qw, qn, gl, wf, bias, s_buf, probs, ds_buf,
           ctx_acc, cb, cw, cf, ct, g_buf, gt_buf, dq_acc, dk_acc, dv_acc, dqw, dqf,
           kvb, rkv, kvs, kvf,
           dw, ry, sx, rx, fr, gf,
           k_rs, v_rs, q_rs, gl_rs, w_rs, c_rs, dq_rs, kv_rs, kvf_rs, y_rs, x_rs, f_rs, z_rs,
           ss, x_ss, z_ss):
    dp = lax.axis_index("dp")
    place = lax.axis_index("ctx")
    xh = lax.div(dp, 2)
    core = lax.rem(dp, 2)
    pair = lax.div(place, 2)
    xl = lax.rem(place, 2)
    y = lax.div(place, 32)
    z = lax.rem(pair, 16)
    group = lax.div(z, 4)
    inner = lax.rem(z, 4)
    spot = y * 2 + xl

    partner = (dp, place + 1 - 2 * xl)
    twin = (dp + 1 - 2 * core, place)
    other = lax.rem(dp + 2, 4)
    across = (other, place + 1 - 2 * xl)
    ahead = (dp, lax.rem(place + 2, PLACES))
    behind = (dp, lax.rem(place + PLACES - 2, PLACES))

    def around(j):
        where = lax.rem(spot + j, 8)
        return (dp, lax.div(where, 2) * 32 + z * 2 + lax.rem(where, 2))

    def quad(x, b):
        return (lax.div(x, 2) * 2 + core, (y * 16 + group * 4 + b) * 2 + lax.rem(x, 2))

    def far(j):
        return (dp, (y * 16 + lax.rem(z + 4 * j, 16)) * 2 + xl)

    barrier = pltpu.get_barrier_semaphore()

    def greet(device):
        pl.semaphore_signal(barrier, inc=1, device_id=device, device_id_type=MESH)

    def greet_quad(j, carry):
        at = lax.rem((xh * 2 + xl) * 4 + inner + j, 16)
        greet(quad(lax.div(at, 4), lax.rem(at, 4)))
        return carry

    def greet_around(j, carry):
        greet(around(j))
        return carry

    def greet_far(j, carry):
        greet(far(j))
        return carry

    for device in (ahead, behind, twin):
        greet(device)
    lax.fori_loop(1, 4, greet_far, 0)
    lax.fori_loop(1, 16, greet_quad, 0)
    lax.fori_loop(1, 8, greet_around, 0)

    own_live = lax.broadcasted_iota(jnp.int32, (ROWS, 128), 0) < cnt_ref[0, place]
    mine = core * 2 + xl
    for block in range(11):
        cols = slice(block * 128, (block + 1) * 128)
        gl[mine, :, cols] = jnp.where(own_live, cot_ref[:, cols].astype(F32), 0.0).astype(BF)

    pl.semaphore_wait(barrier, 28)

    sent = []

    def send(source, target, recv_sem, device):
        copy = pltpu.make_async_remote_copy(
            src_ref=source, dst_ref=target, send_sem=ss.at[len(sent)], recv_sem=recv_sem,
            device_id=device, device_id_type=MESH)
        copy.start()
        sent.append(copy)

    def incoming(ref, recv_sem, send_sem):
        return pltpu.make_async_remote_copy(
            src_ref=ref, dst_ref=ref, send_sem=send_sem, recv_sem=recv_sem,
            device_id=partner, device_id_type=MESH)

    def arrived(ref, recv_sem):
        incoming(ref, recv_sem, ss.at[0]).wait_recv()

    away = 3 - xl
    near_rows = pl.ds(pl.multiple_of(xl * HALF, 16), HALF)
    away_rows = pl.ds(pl.multiple_of((1 - xl) * HALF, 16), HALF)
    send(k_ref.at[away_rows], kw.at[2 + xl], k_rs.at[2 + xl], partner)
    send(k_ref.at[near_rows], kw.at[xl], k_rs.at[xl], ahead)
    send(k_ref.at[near_rows], kw.at[4 + xl], k_rs.at[4 + xl], behind)
    send(v_ref.at[away_rows], vw.at[2 + xl], v_rs.at[2 + xl], partner)
    send(q_ref.at[away_rows], qw.at[xl], q_rs, partner)
    send(gl.at[mine], gl.at[mine], gl_rs.at[mine], partner)
    send(w_ref, wf.at[dp], w_rs.at[dp], across)
    send(w_ref, wf.at[dp], w_rs.at[dp], twin)
    send(gl.at[mine], gl.at[mine], gl_rs.at[mine], twin)
    kw[2 + xl] = k_ref[near_rows, :]
    vw[2 + xl] = v_ref[near_rows, :]
    qw[xl] = q_ref[near_rows, :]

    arrived(kw.at[away], k_rs.at[away])
    send(kw.at[away], kw.at[1 - xl], k_rs.at[1 - xl], ahead)
    send(kw.at[away], kw.at[5 - xl], k_rs.at[5 - xl], behind)
    send(v_ref.at[near_rows], vw.at[xl], v_rs.at[xl], ahead)
    send(v_ref.at[near_rows], vw.at[4 + xl], v_rs.at[4 + xl], behind)
    arrived(vw.at[away], v_rs.at[away])
    send(vw.at[away], vw.at[1 - xl], v_rs.at[1 - xl], ahead)
    send(vw.at[away], vw.at[5 - xl], v_rs.at[5 - xl], behind)

    frames, live = [], []
    for slot in range(SLOTS):
        shard = lax.rem(2 * pair - 2 + slot + PLACES, PLACES)
        inside = (2 * pair - 2 + slot >= 0) & (2 * pair - 2 + slot < PLACES)
        count = jnp.where(inside, cnt_ref[0, shard], 0)
        frame = lax.shift_right_logical(pid_ref[pl.ds(shard, 1), :], 8) + 2 * (slot - 2)
        frames.append(frame.astype(F32))
        live.append(lax.broadcasted_iota(jnp.int32, (ROWS, 128), 1) < count)
    for half in range(2):
        column = jnp.transpose(jnp.broadcast_to(frames[2 + half], (ROWS, 128)))
        for slot in range(SLOTS):
            seen = live[slot] & (jnp.abs(frames[slot] - column) <= WIN)
            bias[half * 128:(half + 1) * 128, slot * 128:(slot + 1) * 128] = jnp.where(seen, 0.0, MASKED)
    wf[dp] = w_ref[...]

    arrived(qw.at[1 - xl], q_rs)
    for half in range(2):
        qn[half * 128:(half + 1) * 128, :] = jnp.transpose(qw[half].astype(F32)).astype(BF)
    for slot in (0, 1, 4, 5):
        arrived(kw.at[slot], k_rs.at[slot])

    def lanes(ref, low, high, first, slots):
        return jnp.concatenate([ref[first + i, low:high, :] for i in range(slots)], axis=1)

    def folded(op, value, old):
        here = op(value[:, :128], value[:, 128:])
        return here if old is None else op(old, here)

    for head in range(4):
        low, high = WINDOWS[head]
        q_head = qn[:, low:high] * head_mask(head, 256).astype(BF)
        top = None
        for part in range(3):
            cols = slice(part * 256, part * 256 + 256)
            score = plain(q_head, lanes(kw, low, high, part * 2, 2)) * SCALE + bias[:, cols]
            s_buf[:, cols] = score
            top = folded(jnp.maximum, score, top)
        top = jnp.max(top, axis=1, keepdims=True)
        total = None
        for part in range(3):
            cols = slice(part * 256, part * 256 + 256)
            expon = jnp.exp(s_buf[:, cols] - top)
            s_buf[:, cols] = expon
            total = folded(jnp.add, expon, total)
        inverse = 1.0 / jnp.sum(total, axis=1, keepdims=True)
        for part in range(3):
            cols = slice(part * 256, part * 256 + 256)
            probs[head, :, cols] = (s_buf[:, cols] * inverse).astype(BF)
        if head == 0:
            for slot in (0, 1, 4, 5):
                arrived(vw.at[slot], v_rs.at[slot])
        ctx_acc[head * HEAD:(head + 1) * HEAD, :] = stripe(
            head, last_last(lanes(vw, *STRIPES[head], 0, SLOTS), probs[head]))
    cb[...] = ctx_acc[...].astype(BF)
    core_rows = pl.ds(pl.multiple_of(core * BLOCK, 16), BLOCK)
    send(cb.at[pl.ds(pl.multiple_of((1 - core) * BLOCK, 16), BLOCK)], ct.at[core], c_rs.at[0], twin)
    cw[0] = cb[:, 0:128]
    cw[1] = cb[:, 128:256]
    send(cw.at[1 - xl], cf.at[near_rows], c_rs.at[1], partner)
    ct[core] = cb[core_rows, :]
    cf[near_rows, :] = cw[xl]

    theirs = core * 2 + 1 - xl
    arrived(gl.at[theirs], gl_rs.at[theirs])
    send(gl.at[theirs], gl.at[theirs], gl_rs.at[theirs], twin)
    arrived(wf.at[other], w_rs.at[other])
    send(wf.at[other], wf.at[other], w_rs.at[other], twin)
    arrived(wf.at[dp + 1 - 2 * core], w_rs.at[dp + 1 - 2 * core])
    arrived(wf.at[other + 1 - 2 * core], w_rs.at[other + 1 - 2 * core])
    grad_context = last_last(gl[pl.ds(core * 2, 2)].reshape(256, D), wf[pl.ds(xl * 2, 2)].reshape(HALF, D))
    g_buf[...] = grad_context.astype(BF)
    gt_buf[...] = jnp.transpose(grad_context).astype(BF)

    arrived(ct.at[1 - core], c_rs.at[0])
    for slot in range(2):
        there = (1 - core) * 2 + slot
        arrived(gl.at[there], gl_rs.at[there])
    context = jnp.concatenate([ct[0], ct[1]], axis=1)
    for start in range(0, D, 256):
        stop = min(start + 256, D)
        part = plain(context, gl[:, :, start:stop].reshape(512, stop - start))
        for column in range(start, stop, 128):
            for row in range(11):
                tile = row * 11 + column // 128
                dw[tile // 32, tile % 32] = part[row * 16:row * 16 + 16, column - start:column - start + 128].astype(BF)
    for tile in range(TILES, 128):
        dw[tile // 32, tile % 32] = jnp.zeros((16, 128), BF)
    for step in (1, 3, 2):
        goal = lax.rem(y + step, 4)
        send(dw.at[goal], ry.at[step - 1], y_rs.at[step - 1], (dp, lax.rem(place + 32 * step, PLACES)))

    for head in range(4):
        low, high = WINDOWS[head]
        g_head = g_buf[:, low:high] * head_mask(head, 256).astype(BF)
        delta = None
        for part in range(3):
            cols = slice(part * 256, part * 256 + 256)
            grad_prob = plain(g_head, lanes(vw, low, high, part * 2, 2))
            s_buf[:, cols] = grad_prob
            delta = folded(jnp.add, probs[head, :, cols].astype(F32) * grad_prob, delta)
        delta = jnp.sum(delta, axis=1, keepdims=True)
        for part in range(3):
            cols = slice(part * 256, part * 256 + 256)
            ds_buf[:, cols] = (probs[head, :, cols].astype(F32) * (s_buf[:, cols] - delta)).astype(BF)
        rows = slice(head * HEAD, (head + 1) * HEAD)
        first, stop = STRIPES[head]
        dk_acc[rows, :] = stripe(head, plain(lanes(qw, first, stop, 0, 2), ds_buf[...])) * SCALE
        dv_acc[rows, :] = stripe(head, plain(gt_buf[first:stop, :], probs[head]))
        dq_acc[rows, :] = stripe(head, last_last(lanes(kw, first, stop, 0, SLOTS), ds_buf[...])) * SCALE
        if head % 2 == 1:
            piece = head // 2
            block = slice(piece * BLOCK, (piece + 1) * BLOCK)
            for side in range(2):
                cols = slice(side * 512, side * 512 + 256)
                kvb[side, piece, 0] = dk_acc[block, cols].astype(BF)
                kvb[side, piece, 1] = dv_acc[block, cols].astype(BF)
                send(kvb.at[side, piece], rkv.at[1 - side, piece], kv_rs.at[1 - side, piece], (behind, ahead)[side])
    dqw[0] = dq_acc[:, 0:128].astype(BF)
    dqw[1] = dq_acc[:, 128:256].astype(BF)
    send(dqw.at[1 - xl], dqf, dq_rs, partner)
    gq_ref[near_rows, :] = dqw[xl]

    for step in range(3):
        arrived(ry.at[step], y_rs.at[step])
    total = dw[y].astype(F32) + ry[0].astype(F32) + ry[1].astype(F32) + ry[2].astype(F32)
    sx[...] = total.astype(BF).reshape(8, 4, 16, 128)

    def stays(half, b):
        return (xh == xl) & (xl == half) & (inner == b)

    def quad_copy(n):
        half, b = lax.div(n, 4), lax.rem(n, 4)
        return pltpu.make_async_remote_copy(
            src_ref=sx.at[n], dst_ref=rx.at[xh * 4 + inner], send_sem=x_ss.at[n], recv_sem=x_rs.at[xh * 4 + inner],
            device_id=quad(xl * 2 + half, b), device_id_type=MESH)

    def quad_start(n, carry):
        @pl.when(jnp.logical_not(stays(lax.div(n, 4), lax.rem(n, 4))))
        def _():
            quad_copy(n).start()

        return carry

    def quad_sent(n, carry):
        @pl.when(jnp.logical_not(stays(lax.div(n, 4), lax.rem(n, 4))))
        def _():
            quad_copy(n).wait_send()

        return carry

    def quad_here(n, carry):
        @pl.when(jnp.logical_not((xh == xl) & (n == xh * 4 + inner)))
        def _():
            arrived(rx.at[n], x_rs.at[n])

        return carry

    lax.fori_loop(0, 8, quad_start, 0)

    @pl.when(xh == xl)
    def _():
        rx[xh * 4 + inner] = sx[xl * 4 + inner]

    arrived(cf.at[away_rows], c_rs.at[1])
    projected = first_first(cf[...], wf[...].reshape(HW, D))
    for block in range(11):
        cols = slice(block * 128, (block + 1) * 128)
        att_ref[:, cols] = jnp.where(own_live, projected[:, cols], 0.0).astype(BF)

    lax.fori_loop(0, 8, quad_here, 0)
    total = rx[0].astype(F32)
    for source in range(1, 8):
        total = total + rx[source].astype(F32)
    fr[group] = total.astype(BF)
    for step in (2, 1, 3):
        send(fr.at[group], fr.at[group], f_rs.at[group], far(step))

    for piece in range(2):
        block = slice(piece * BLOCK, (piece + 1) * BLOCK)
        for side in range(2):
            arrived(rkv.at[side, piece], kv_rs.at[side, piece])
        for which, acc in ((0, dk_acc), (1, dv_acc)):
            value = acc[block, 256:512] + rkv[0, piece, which].astype(F32) + rkv[1, piece, which].astype(F32)
            kvs[0, which, block, :] = value[:, 0:128].astype(BF)
            kvs[1, which, block, :] = value[:, 128:256].astype(BF)
    send(kvs.at[1 - xl], kvf, kvf_rs, partner)
    gk_ref[near_rows, :] = kvs[xl, 0]
    gv_ref[near_rows, :] = kvs[xl, 1]
    arrived(dqf, dq_rs)
    gq_ref[away_rows, :] = dqf[...]

    for step in range(1, 4):
        source = lax.rem(group + step, 4)
        arrived(fr.at[source], f_rs.at[source])
    total = fr[0].astype(F32) + fr[1].astype(F32) + fr[2].astype(F32) + fr[3].astype(F32)
    gf[spot, inner] = total.astype(BF)

    def spread(j, carry):
        pltpu.make_async_remote_copy(
            src_ref=gf.at[spot, inner], dst_ref=gf.at[spot, inner], send_sem=z_ss.at[0], recv_sem=z_rs.at[0],
            device_id=quad(xh * 2 + xl, lax.rem(inner + j, 4)), device_id_type=MESH).start()
        return carry

    def share(j, carry):
        pltpu.make_async_remote_copy(
            src_ref=gf.at[spot], dst_ref=gf.at[spot], send_sem=z_ss.at[1], recv_sem=z_rs.at[1],
            device_id=around(j), device_id_type=MESH).start()
        return carry

    three = incoming(gf.at[0, pl.ds(0, 3)], z_rs.at[0], z_ss.at[0])
    seven = incoming(gf.at[pl.ds(0, 7)], z_rs.at[1], z_ss.at[1])
    lax.fori_loop(1, 4, spread, 0)
    three.wait_recv()
    lax.fori_loop(1, 8, share, 0)

    arrived(kvf, kvf_rs)
    gk_ref[away_rows, :] = kvf[0]
    gv_ref[away_rows, :] = kvf[1]

    seven.wait_recv()
    for tile in range(TILES):
        row, column = tile // 11, tile % 11
        gw_ref[row * 16:row * 16 + 16, column * 128:(column + 1) * 128] = gf[
            tile // 16, tile // 4 % 4, tile % 4].astype(F32)

    for copy in sent:
        copy.wait_send()
    lax.fori_loop(0, 8, quad_sent, 0)
    three.wait_send()
    seven.wait_send()


def hand_over(*refs):
    count = len(refs) // 2
    sems = refs[-1]
    copies = [pltpu.make_async_copy(refs[i], refs[count + i], sems.at[i]) for i in range(count)]
    for copy in copies:
        copy.start()
    for copy in copies:
        copy.wait()


def per_device(queries, keys, values, patch_ids, counts, cotangent, w_out):
    vmem = pl.BlockSpec(memory_space=pltpu.VMEM)
    smem = pl.BlockSpec(memory_space=pltpu.SMEM)
    whole = pl.BlockSpec(memory_space=pl.ANY)
    halves = (2, HALF, ROWS)
    window = (SLOTS, HALF, ROWS)
    dma = pltpu.SemaphoreType.DMA
    scratch = [
        pltpu.VMEM(window, BF), pltpu.VMEM(window, BF), pltpu.VMEM(halves, BF), pltpu.VMEM((256, HALF), BF),
        pltpu.VMEM((4, ROWS, D), BF), pltpu.VMEM((4, BLOCK, D), BF),
        pltpu.VMEM((256, 768), F32), pltpu.VMEM((256, 768), F32),
        pltpu.VMEM((4, 256, 768), BF), pltpu.VMEM((256, 768), BF),
        pltpu.VMEM((HALF, 256), F32), pltpu.VMEM((HALF, 256), BF), pltpu.VMEM(halves, BF), pltpu.VMEM((HW, ROWS), BF),
        pltpu.VMEM((2, BLOCK, 256), BF), pltpu.VMEM((256, HALF), BF), pltpu.VMEM((HALF, 256), BF),
        pltpu.VMEM((HALF, 256), F32), pltpu.VMEM((HALF, 768), F32), pltpu.VMEM((HALF, 768), F32),
        pltpu.VMEM(halves, BF), pltpu.VMEM((HALF, ROWS), BF),
        pltpu.VMEM((2, 2, 2, BLOCK, 256), BF), pltpu.VMEM((2, 2, 2, BLOCK, 256), BF),
        pltpu.VMEM((2, 2, HALF, ROWS), BF), pltpu.VMEM((2, HALF, ROWS), BF),
        pltpu.VMEM((4, 32, 16, 128), BF), pltpu.VMEM((3, 32, 16, 128), BF),
        pltpu.VMEM((8, 4, 16, 128), BF), pltpu.VMEM((8, 4, 16, 128), BF),
        pltpu.VMEM((4, 4, 16, 128), BF), pltpu.VMEM((8, 4, 4, 16, 128), BF),
        dma((6,)), dma((6,)), dma, dma((4,)), dma((4,)), dma((2,)), dma, dma((2, 2)), dma, dma((3,)), dma((8,)),
        dma((4,)), dma((2,)),
        dma((40,)), dma((8,)), dma((2,)),
    ]
    shapes = (
        jax.ShapeDtypeStruct((ROWS, D), BF),
        jax.ShapeDtypeStruct((HW, ROWS), BF),
        jax.ShapeDtypeStruct((HW, ROWS), BF),
        jax.ShapeDtypeStruct((HW, ROWS), BF),
        jax.ShapeDtypeStruct((BLOCK, D), F32),
    )
    outs = pl.pallas_call(
        kernel,
        out_shape=shapes,
        in_specs=[vmem, vmem, vmem, vmem, smem, vmem, vmem],
        out_specs=(vmem,) * 5,
        scratch_shapes=scratch,
        compiler_params=pltpu.CompilerParams(
            collective_id=0, has_side_effects=True, vmem_limit_bytes=48 * 1024 * 1024),
        cost_estimate=pl.CostEstimate(flops=1500000000, bytes_accessed=4000000, transcendentals=800000),
    )(queries[0].T, keys[0].T, values[0].T, patch_ids.reshape(PLACES, ROWS), counts, cotangent[0], w_out)
    outs = pl.pallas_call(
        hand_over,
        out_shape=shapes,
        in_specs=[whole] * 5,
        out_specs=(whole,) * 5,
        scratch_shapes=[dma((5,))],
    )(*outs)
    attended, grad_queries, grad_keys, grad_values, grad_weight = outs
    return attended[None], grad_queries.T[None], grad_keys.T[None], grad_values.T[None], grad_weight


def solution(mesh):
    placed = (
        P("dp", "ctx", None),
        P("dp", "ctx", None),
        P("dp", "ctx", None),
        P("dp", None),
        P("dp", None),
        P("dp", "ctx", None),
        P("dp", None),
    )
    return jax.shard_map(
        per_device,
        mesh=mesh,
        in_specs=placed,
        out_specs=(
            P("dp", "ctx", None),
            P("dp", "ctx", None),
            P("dp", "ctx", None),
            P("dp", "ctx", None),
            P("dp", None),
        ),
        check_vma=False,
    )
```

time: 87.2 us -> 140 us (1.61)
  the two profiles are of different devices: /device:TPU:6 before, /device:TPU:1 now
where the time goes in v2:
time: 140 us; the launch traced here: 139 us
  Pallas kernels  129 us (92%)
  local copies, waits for them, and re-layouts  9.96 us (7%)
    pallas_call x1, Pallas kernels, per_device(): pl.pallas_call(kernel, out_shape=shapes, in_specs=[vmem, vmem, vmem, vmem...  70.4 us
    pallas_call x1, Pallas kernels, per_device(): pl.pallas_call(hand_over, out_shape=shapes, in_specs=[whole] * 5, out_spe...  58.5 us
    unnamed x24, local copies, waits for them, and re-layouts  9.96 us

profile of v2, /device:TPU:1, one launch (start us, length us, event | category | flops | bytes accessed | tf_op | source)
XLA Modules:
  0.0 139.5 jit_solution(16301807529038346271)
XLA Ops:
  0.6 0.0 copy-start.11
  0.6 0.6 copy-done.11
  1.3 0.0 copy-start.5
  1.3 1.0 copy-done.5
  2.3 0.0 copy-start.6
  2.3 1.0 copy-done.6
  3.3 0.0 copy-start.7
  3.3 0.9 copy-done.7
  4.2 0.0 copy-start.8
  4.2 0.9 copy-done.8
  5.2 0.0 copy-start.9
  5.2 0.9 copy-done.9
  6.1 0.0 copy-start.10
  6.1 0.8 copy-done.10
  6.9 70.4 %shard_map.110 = (bf16[128,1408]{1,0:T(8,128)(2,1)S(1)}, bf16[704,128]{1,0:T(8,128)(2,1)S(1)}, bf16[704,128]{1,0:T(8,128)(2,1)S(1)}, bf16[704,128]{1,0:T(8,128)(2,1)S(1)}, f32[176,1408]{1,0:T(8,128)S(1)}) custom-call(bf16[704,128]{1,0:T(8,128)(2,1)S(1)} %bitcast.22, bf16[704,128]{1,0:T(8,128)(2,1)S(1)} %bitcast.23, bf16[704,128]{1,0:T(8,128)(2,1)S(1)} %bitcast.24, ...), custom_call_target="tpu_custom_call" | custom-call | flops 1500000000 | bytes 4000000 | tf_op jit(solution)/shard_map/pallas_call | solution.py:435
  77.3 0.0 copy-start
  77.3 0.9 copy-done
  78.3 0.0 copy-start.1
  78.3 0.8 copy-done.1
  79.0 0.0 copy-start.2
  79.0 0.7 copy-done.2
  79.7 0.7 copy-done.3
  80.4 0.7 copy-done.4
  81.0 58.5 %shard_map.111 = (bf16[128,1408]{1,0:T(8,128)(2,1)}, bf16[704,128]{1,0:T(8,128)(2,1)}, bf16[704,128]{1,0:T(8,128)(2,1)}, bf16[704,128]{1,0:T(8,128)(2,1)}, f32[176,1408]{1,0:T(8,128)}) custom-call(bf16[128,1408]{1,0:T(8,128)(2,1)} %copy-done.1, bf16[704,128]{1,0:T(8,128)(2,1)} %copy-done.2, bf16[704,128]{1,0:T(8,128)(2,1)} %copy-done.3, ...), custom_call_target="tpu_custom_call" | custom-call | tf_op jit(solution)/shard_map/pallas_call | solution.py:445
  (2 shorter events, 0.0 us)
Async XLA Ops:
  0.6 0.7 copy-start.11
  1.3 1.0 copy-start.5
  2.3 1.0 copy-start.6
  3.3 0.9 copy-start.7
  4.2 0.9 copy-start.8
  5.2 0.9 copy-start.9
  6.1 0.8 copy-start.10
  77.3 1.0 copy-start
  78.3 0.8 copy-start.1
  79.0 0.7 copy-start.2
  79.7 0.7 copy-start.3
  80.4 0.7 copy-start.4

commit v3 on v2

--- a/solution.py
+++ b/solution.py
@@ -17,6 +17,7 @@
 SCALE = HEAD ** -0.5
 MASKED = -1e30
 TILES = 121
+VMEM_LIMIT = 61 * 1024 * 1024
 MESH = pl.DeviceIdType.MESH
 WINDOWS = ((0, 128), (0, 256), (128, 352), (256, 352))
 STRIPES = ((0, 96), (80, 176), (176, 272), (256, 352))
@@ -47,14 +48,15 @@
     return value[skip:skip + HEAD]
 
 
-def kernel(q_ref, k_ref, v_ref, pid_ref, cnt_ref, cot_ref, w_ref,
-           att_ref, gq_ref, gk_ref, gv_ref, gw_ref,
+def kernel(q_ref, k_ref, v_ref, pid_hbm, cnt_hbm, cot_hbm, w_ref,
+           att_hbm, gq_hbm, gk_hbm, gv_hbm, gw_hbm,
+           pid_ref, cnt_ref, cot_ref, att_ref,
            kw, vw, qw, qn, gl, wf, bias, s_buf, probs, ds_buf,
            ctx_acc, cb, cw, cf, ct, g_buf, gt_buf, dq_acc, dk_acc, dv_acc, dqw, dqf,
            kvb, rkv, kvs, kvf,
            dw, ry, sx, rx, fr, gf,
            k_rs, v_rs, q_rs, gl_rs, w_rs, c_rs, dq_rs, kv_rs, kvf_rs, y_rs, x_rs, f_rs, z_rs,
-           ss, x_ss, z_ss):
+           ss, x_ss, z_ss, in_sems, out_sems):
     dp = lax.axis_index("dp")
     place = lax.axis_index("ctx")
     xh = lax.div(dp, 2)
@@ -84,6 +86,21 @@
     def far(j):
         return (dp, (y * 16 + lax.rem(z + 4 * j, 16)) * 2 + xl)
 
+    near_rows = pl.ds(pl.multiple_of(xl * HALF, 16), HALF)
+    away_rows = pl.ds(pl.multiple_of((1 - xl) * HALF, 16), HALF)
+    fetches = []
+    for source, target in (
+            (cot_hbm, cot_ref), (cnt_hbm, cnt_ref), (pid_hbm, pid_ref), (k_ref.at[near_rows], kw.at[2 + xl]),
+            (q_ref.at[near_rows], qw.at[xl]), (v_ref.at[near_rows], vw.at[2 + xl]), (w_ref, wf.at[dp])):
+        fetches.append(pltpu.make_async_copy(source, target, in_sems.at[len(fetches)]))
+        fetches[-1].start()
+
+    written = []
+
+    def write(source, target):
+        written.append(pltpu.make_async_copy(source, target, out_sems.at[len(written)]))
+        written[-1].start()
+
     barrier = pltpu.get_barrier_semaphore()
 
     def greet(device):
@@ -108,6 +125,8 @@
     lax.fori_loop(1, 16, greet_quad, 0)
     lax.fori_loop(1, 8, greet_around, 0)
 
+    fetches[0].wait()
+    fetches[1].wait()
     own_live = lax.broadcasted_iota(jnp.int32, (ROWS, 128), 0) < cnt_ref[0, place]
     mine = core * 2 + xl
     for block in range(11):
@@ -134,8 +153,6 @@
         incoming(ref, recv_sem, ss.at[0]).wait_recv()
 
     away = 3 - xl
-    near_rows = pl.ds(pl.multiple_of(xl * HALF, 16), HALF)
-    away_rows = pl.ds(pl.multiple_of((1 - xl) * HALF, 16), HALF)
     send(k_ref.at[away_rows], kw.at[2 + xl], k_rs.at[2 + xl], partner)
     send(k_ref.at[near_rows], kw.at[xl], k_rs.at[xl], ahead)
     send(k_ref.at[near_rows], kw.at[4 + xl], k_rs.at[4 + xl], behind)
@@ -145,9 +162,8 @@
     send(w_ref, wf.at[dp], w_rs.at[dp], across)
     send(w_ref, wf.at[dp], w_rs.at[dp], twin)
     send(gl.at[mine], gl.at[mine], gl_rs.at[mine], twin)
-    kw[2 + xl] = k_ref[near_rows, :]
-    vw[2 + xl] = v_ref[near_rows, :]
-    qw[xl] = q_ref[near_rows, :]
+    for fetch in fetches[2:]:
+        fetch.wait()
 
     arrived(kw.at[away], k_rs.at[away])
     send(kw.at[away], kw.at[1 - xl], k_rs.at[1 - xl], ahead)
@@ -171,7 +187,6 @@
         for slot in range(SLOTS):
             seen = live[slot] & (jnp.abs(frames[slot] - column) <= WIN)
             bias[half * 128:(half + 1) * 128, slot * 128:(slot + 1) * 128] = jnp.where(seen, 0.0, MASKED)
-    wf[dp] = w_ref[...]
 
     arrived(qw.at[1 - xl], q_rs)
     for half in range(2):
@@ -278,7 +293,7 @@
     dqw[0] = dq_acc[:, 0:128].astype(BF)
     dqw[1] = dq_acc[:, 128:256].astype(BF)
     send(dqw.at[1 - xl], dqf, dq_rs, partner)
-    gq_ref[near_rows, :] = dqw[xl]
+    write(dqw.at[xl], gq_hbm.at[near_rows])
 
     for step in range(3):
         arrived(ry.at[step], y_rs.at[step])
@@ -326,6 +341,7 @@
     for block in range(11):
         cols = slice(block * 128, (block + 1) * 128)
         att_ref[:, cols] = jnp.where(own_live, projected[:, cols], 0.0).astype(BF)
+    write(att_ref, att_hbm)
 
     lax.fori_loop(0, 8, quad_here, 0)
     total = rx[0].astype(F32)
@@ -344,10 +360,10 @@
             kvs[0, which, block, :] = value[:, 0:128].astype(BF)
             kvs[1, which, block, :] = value[:, 128:256].astype(BF)
     send(kvs.at[1 - xl], kvf, kvf_rs, partner)
-    gk_ref[near_rows, :] = kvs[xl, 0]
-    gv_ref[near_rows, :] = kvs[xl, 1]
+    write(kvs.at[xl, 0], gk_hbm.at[near_rows])
+    write(kvs.at[xl, 1], gv_hbm.at[near_rows])
     arrived(dqf, dq_rs)
-    gq_ref[away_rows, :] = dqf[...]
+    write(dqf, gq_hbm.at[away_rows])
 
     for step in range(1, 4):
         source = lax.rem(group + step, 4)
@@ -374,40 +390,52 @@
     lax.fori_loop(1, 8, share, 0)
 
     arrived(kvf, kvf_rs)
-    gk_ref[away_rows, :] = kvf[0]
-    gv_ref[away_rows, :] = kvf[1]
+    write(kvf.at[0], gk_hbm.at[away_rows])
+    write(kvf.at[1], gv_hbm.at[away_rows])
 
     seven.wait_recv()
-    for tile in range(TILES):
-        row, column = tile // 11, tile % 11
-        gw_ref[row * 16:row * 16 + 16, column * 128:(column + 1) * 128] = gf[
-            tile // 16, tile // 4 % 4, tile % 4].astype(F32)
-
+    write(gf, gw_hbm)
     for copy in sent:
         copy.wait_send()
     lax.fori_loop(0, 8, quad_sent, 0)
     three.wait_send()
     seven.wait_send()
-
-
-def hand_over(*refs):
-    count = len(refs) // 2
-    sems = refs[-1]
-    copies = [pltpu.make_async_copy(refs[i], refs[count + i], sems.at[i]) for i in range(count)]
-    for copy in copies:
+    for copy in written:
+        copy.wait()
+
+
+def hand_over(att_in, gq_in, gk_in, gv_in, gw_in, att_out, gq_out, gk_out, gv_out, gw_out,
+              att, gq, gk, gv, tiles, gw, in_sems, out_sems):
+    held = (tiles, att, gq, gk, gv)
+    outs = (gw_out, att_out, gq_out, gk_out, gv_out)
+    reads = [pltpu.make_async_copy(source, target, in_sems.at[i])
+             for i, (source, target) in enumerate(zip((gw_in, att_in, gq_in, gk_in, gv_in), held))]
+    writes = [pltpu.make_async_copy(source, target, out_sems.at[i])
+              for i, (source, target) in enumerate(zip((gw,) + held[1:], outs))]
+    for read in reads:
+        read.start()
+    for read, copy in list(zip(reads, writes))[1:]:
+        read.wait()
         copy.start()
-    for copy in copies:
+    reads[0].wait()
+    for tile in range(TILES):
+        row, column = tile // 11, tile % 11
+        gw[row * 16:row * 16 + 16, column * 128:(column + 1) * 128] = tiles[
+            tile // 16, tile // 4 % 4, tile % 4].astype(F32)
+    writes[0].start()
+    for copy in writes:
         copy.wait()
 
 
 def per_device(queries, keys, values, patch_ids, counts, cotangent, w_out):
-    vmem = pl.BlockSpec(memory_space=pltpu.VMEM)
-    smem = pl.BlockSpec(memory_space=pltpu.SMEM)
-    whole = pl.BlockSpec(memory_space=pl.ANY)
+    hbm = pl.BlockSpec(memory_space=pltpu.HBM)
+    tiles = (8, 4, 4, 16, 128)
     halves = (2, HALF, ROWS)
     window = (SLOTS, HALF, ROWS)
     dma = pltpu.SemaphoreType.DMA
     scratch = [
+        pltpu.VMEM((PLACES, ROWS), jnp.int32), pltpu.SMEM((1, PLACES), jnp.int32), pltpu.VMEM((ROWS, D), BF),
+        pltpu.VMEM((ROWS, D), BF),
         pltpu.VMEM(window, BF), pltpu.VMEM(window, BF), pltpu.VMEM(halves, BF), pltpu.VMEM((256, HALF), BF),
         pltpu.VMEM((4, ROWS, D), BF), pltpu.VMEM((4, BLOCK, D), BF),
         pltpu.VMEM((256, 768), F32), pltpu.VMEM((256, 768), F32),
@@ -420,34 +448,36 @@
         pltpu.VMEM((2, 2, HALF, ROWS), BF), pltpu.VMEM((2, HALF, ROWS), BF),
         pltpu.VMEM((4, 32, 16, 128), BF), pltpu.VMEM((3, 32, 16, 128), BF),
         pltpu.VMEM((8, 4, 16, 128), BF), pltpu.VMEM((8, 4, 16, 128), BF),
-        pltpu.VMEM((4, 4, 16, 128), BF), pltpu.VMEM((8, 4, 4, 16, 128), BF),
+        pltpu.VMEM((4, 4, 16, 128), BF), pltpu.VMEM(tiles, BF),
         dma((6,)), dma((6,)), dma, dma((4,)), dma((4,)), dma((2,)), dma, dma((2, 2)), dma, dma((3,)), dma((8,)),
         dma((4,)), dma((2,)),
-        dma((40,)), dma((8,)), dma((2,)),
+        dma((40,)), dma((8,)), dma((2,)), dma((7,)), dma((8,)),
     ]
     shapes = (
         jax.ShapeDtypeStruct((ROWS, D), BF),
         jax.ShapeDtypeStruct((HW, ROWS), BF),
         jax.ShapeDtypeStruct((HW, ROWS), BF),
         jax.ShapeDtypeStruct((HW, ROWS), BF),
-        jax.ShapeDtypeStruct((BLOCK, D), F32),
     )
     outs = pl.pallas_call(
         kernel,
-        out_shape=shapes,
-        in_specs=[vmem, vmem, vmem, vmem, smem, vmem, vmem],
-        out_specs=(vmem,) * 5,
+        out_shape=shapes + (jax.ShapeDtypeStruct(tiles, BF),),
+        in_specs=[hbm] * 7,
+        out_specs=(hbm,) * 5,
         scratch_shapes=scratch,
         compiler_params=pltpu.CompilerParams(
-            collective_id=0, has_side_effects=True, vmem_limit_bytes=48 * 1024 * 1024),
+            collective_id=0, has_side_effects=True, vmem_limit_bytes=VMEM_LIMIT),
         cost_estimate=pl.CostEstimate(flops=1500000000, bytes_accessed=4000000, transcendentals=800000),
     )(queries[0].T, keys[0].T, values[0].T, patch_ids.reshape(PLACES, ROWS), counts, cotangent[0], w_out)
     outs = pl.pallas_call(
         hand_over,
-        out_shape=shapes,
-        in_specs=[whole] * 5,
-        out_specs=(whole,) * 5,
-        scratch_shapes=[dma((5,))],
+        out_shape=shapes + (jax.ShapeDtypeStruct((BLOCK, D), F32),),
+        in_specs=[hbm] * 5,
+        out_specs=(hbm,) * 5,
+        scratch_shapes=[
+            pltpu.VMEM((ROWS, D), BF), pltpu.VMEM((HW, ROWS), BF), pltpu.VMEM((HW, ROWS), BF), pltpu.VMEM((HW, ROWS), BF),
+            pltpu.VMEM(tiles, BF), pltpu.VMEM((BLOCK, D), F32), dma((5,)), dma((5,))],
+        compiler_params=pltpu.CompilerParams(vmem_limit_bytes=VMEM_LIMIT),
     )(*outs)
     attended, grad_queries, grad_keys, grad_values, grad_weight = outs
     return attended[None], grad_queries.T[None], grad_keys.T[None], grad_values.T[None], grad_weight

time: 140 us -> 74.1 us (0.53)
  Pallas kernels: 129 us -> 73.3 us
  local copies, waits for them, and re-layouts: 9.96 us -> 0 us
    pallas_call x2, Pallas kernels: 129 us -> 73.3 us  [the longest x1 70.8 us: per_device(): pl.pallas_call(kernel, out_shape=shapes + (jax.ShapeDtypeStruct(tiles, BF...]
    unnamed x24 -> x0, local copies, waits for them, and re-layouts: 9.96 us -> none
where the time goes in v3:
time: 74.1 us; the launch traced here: 73.9 us
  Pallas kernels  73.3 us (99%)
    pallas_call x1, Pallas kernels, per_device(): pl.pallas_call(kernel, out_shape=shapes + (jax.ShapeDtypeStruct(tiles, BF...  70.8 us
    pallas_call x1, Pallas kernels, per_device(): pl.pallas_call(hand_over, out_shape=shapes + (jax.ShapeDtypeStruct((BLOCK...  2.48 us

profile of v3, /device:TPU:1, one launch (start us, length us, event | category | flops | bytes accessed | tf_op | source)
XLA Modules:
  0.0 73.9 jit_solution(17043034240275305117)
XLA Ops:
  0.6 70.8 %shard_map.110 = (bf16[128,1408]{1,0:T(8,128)(2,1)}, bf16[704,128]{1,0:T(8,128)(2,1)}, bf16[704,128]{1,0:T(8,128)(2,1)}, bf16[704,128]{1,0:T(8,128)(2,1)}, bf16[8,4,4,16,128]{4,3,2,1,0:T(8,128)(2,1)}) custom-call(bf16[704,128]{1,0:T(8,128)(2,1)} %bitcast.23, bf16[704,128]{1,0:T(8,128)(2,1)} %bitcast.24, bf16[704,128]{1,0:T(8,128)(2,1)} %bitcast.25, ...), custom_call_target="tpu_custom_call" | custom-call | flops 1500000000 | bytes 4000000 | tf_op jit(solution)/shard_map/pallas_call | solution.py:462
  71.4 2.5 %shard_map.111 = (bf16[128,1408]{1,0:T(8,128)(2,1)}, bf16[704,128]{1,0:T(8,128)(2,1)}, bf16[704,128]{1,0:T(8,128)(2,1)}, bf16[704,128]{1,0:T(8,128)(2,1)}, f32[176,1408]{1,0:T(8,128)}) custom-call(bf16[128,1408]{1,0:T(8,128)(2,1)} %get-tuple-element.15.att_in, bf16[704,128]{1,0:T(8,128)(2,1)} %get-tuple-element.16.gq_in, ...), custom_call_target="tpu_custom_call" | custom-call | tf_op jit(solution)/shard_map/pallas_call | solution.py:472

commit v4 on v3

--- a/solution.py
+++ b/solution.py
@@ -17,6 +17,8 @@
 SCALE = HEAD ** -0.5
 MASKED = -1e30
 TILES = 121
+PIECE = 384
+ORDER = (1, 3, 2, 0)
 VMEM_LIMIT = 61 * 1024 * 1024
 MESH = pl.DeviceIdType.MESH
 WINDOWS = ((0, 128), (0, 256), (128, 352), (256, 352))
@@ -54,9 +56,9 @@
            kw, vw, qw, qn, gl, wf, bias, s_buf, probs, ds_buf,
            ctx_acc, cb, cw, cf, ct, g_buf, gt_buf, dq_acc, dk_acc, dv_acc, dqw, dqf,
            kvb, rkv, kvs, kvf,
-           dw, ry, sx, rx, fr, gf,
-           k_rs, v_rs, q_rs, gl_rs, w_rs, c_rs, dq_rs, kv_rs, kvf_rs, y_rs, x_rs, f_rs, z_rs,
-           ss, x_ss, z_ss, in_sems, out_sems):
+           dw, dwx, ry, ryx, sx, rx, fr, gf,
+           k_rs, v_rs, q_rs, gl_rs, w_rs, c_rs, dq_rs, kv_rs, kvf_rs, y_rs, yx_rs, x_rs, f_rs, z_rs,
+           ss, y_ss, x_ss, z_ss, in_sems, out_sems):
     dp = lax.axis_index("dp")
     place = lax.axis_index("ctx")
     xh = lax.div(dp, 2)
@@ -131,7 +133,12 @@
     mine = core * 2 + xl
     for block in range(11):
         cols = slice(block * 128, (block + 1) * 128)
-        gl[mine, :, cols] = jnp.where(own_live, cot_ref[:, cols].astype(F32), 0.0).astype(BF)
+        inside = slice(block % 3 * 128, (block % 3 + 1) * 128)
+        gl[block // 3, mine, :, inside] = jnp.where(own_live, cot_ref[:, cols].astype(F32), 0.0).astype(BF)
+    gl[3, mine, :, 256:384] = jnp.zeros((ROWS, 128), BF)
+
+    def piece_at(step):
+        return lax.rem(y + step, 4)
 
     pl.semaphore_wait(barrier, 28)
 
@@ -157,19 +164,21 @@
     send(k_ref.at[near_rows], kw.at[xl], k_rs.at[xl], ahead)
     send(k_ref.at[near_rows], kw.at[4 + xl], k_rs.at[4 + xl], behind)
     send(v_ref.at[away_rows], vw.at[2 + xl], v_rs.at[2 + xl], partner)
+    send(v_ref.at[near_rows], vw.at[xl], v_rs.at[xl], ahead)
+    send(v_ref.at[near_rows], vw.at[4 + xl], v_rs.at[4 + xl], behind)
     send(q_ref.at[away_rows], qw.at[xl], q_rs, partner)
-    send(gl.at[mine], gl.at[mine], gl_rs.at[mine], partner)
+    for step in ORDER:
+        here = gl.at[piece_at(step), mine]
+        send(here, here, gl_rs.at[mine, step], partner)
     send(w_ref, wf.at[dp], w_rs.at[dp], across)
     send(w_ref, wf.at[dp], w_rs.at[dp], twin)
-    send(gl.at[mine], gl.at[mine], gl_rs.at[mine], twin)
+    send(gl.at[:, mine], gl.at[:, mine], gl_rs.at[mine, 0], twin)
     for fetch in fetches[2:]:
         fetch.wait()
 
     arrived(kw.at[away], k_rs.at[away])
     send(kw.at[away], kw.at[1 - xl], k_rs.at[1 - xl], ahead)
     send(kw.at[away], kw.at[5 - xl], k_rs.at[5 - xl], behind)
-    send(v_ref.at[near_rows], vw.at[xl], v_rs.at[xl], ahead)
-    send(v_ref.at[near_rows], vw.at[4 + xl], v_rs.at[4 + xl], behind)
     arrived(vw.at[away], v_rs.at[away])
     send(vw.at[away], vw.at[1 - xl], v_rs.at[1 - xl], ahead)
     send(vw.at[away], vw.at[5 - xl], v_rs.at[5 - xl], behind)
@@ -200,6 +209,13 @@
     def folded(op, value, old):
         here = op(value[:, :128], value[:, 128:])
         return here if old is None else op(old, here)
+
+    theirs = core * 2 + 1 - xl
+
+    def relay_cotangent(step):
+        here = gl.at[piece_at(step), theirs]
+        arrived(here, gl_rs.at[theirs, step])
+        send(here, here, gl_rs.at[theirs, step], twin)
 
     for head in range(4):
         low, high = WINDOWS[head]
@@ -221,9 +237,10 @@
         for part in range(3):
             cols = slice(part * 256, part * 256 + 256)
             probs[head, :, cols] = (s_buf[:, cols] * inverse).astype(BF)
-        if head == 0:
-            for slot in (0, 1, 4, 5):
-                arrived(vw.at[slot], v_rs.at[slot])
+    relay_cotangent(ORDER[0])
+    for slot in (0, 1, 4, 5):
+        arrived(vw.at[slot], v_rs.at[slot])
+    for head in range(4):
         ctx_acc[head * HEAD:(head + 1) * HEAD, :] = stripe(
             head, last_last(lanes(vw, *STRIPES[head], 0, SLOTS), probs[head]))
     cb[...] = ctx_acc[...].astype(BF)
@@ -235,36 +252,116 @@
     ct[core] = cb[core_rows, :]
     cf[near_rows, :] = cw[xl]
 
-    theirs = core * 2 + 1 - xl
-    arrived(gl.at[theirs], gl_rs.at[theirs])
-    send(gl.at[theirs], gl.at[theirs], gl_rs.at[theirs], twin)
+    def weight_piece(step):
+        piece = piece_at(step)
+        there = (1 - core) * 2 + 1 - xl
+        arrived(gl.at[piece, there], gl_rs.at[there, step])
+        part = plain(context, gl[piece].reshape(512, PIECE))
+        for tile in range(33):
+            row, column = tile % 11 * 16, tile // 11 * 128
+            value = part[row:row + 16, column:column + 128].astype(BF)
+            if tile < 32:
+                dw[piece, tile] = value
+            else:
+                dwx[piece] = value
+        if step:
+            send(dw.at[piece], ry.at[step - 1], y_rs.at[step - 1], (dp, piece * 32 + z * 2 + xl))
+
+    def extra_copy():
+        return pltpu.make_async_remote_copy(
+            src_ref=dwx.at[pl.ds(0, 3)], dst_ref=ryx.at[y], send_sem=y_ss, recv_sem=yx_rs.at[y],
+            device_id=(dp, 96 + z * 2 + xl), device_id_type=MESH)
+
+    relay_cotangent(ORDER[1])
+    arrived(gl.at[:, (1 - core) * 2 + xl], gl_rs.at[(1 - core) * 2 + xl, 0])
+    arrived(ct.at[1 - core], c_rs.at[0])
+    context = jnp.concatenate([ct[0], ct[1]], axis=1)
+    weight_piece(ORDER[0])
+    weight_piece(ORDER[1])
     arrived(wf.at[other], w_rs.at[other])
     send(wf.at[other], wf.at[other], w_rs.at[other], twin)
+    relay_cotangent(ORDER[2])
+    weight_piece(ORDER[2])
+
+    arrived(cf.at[away_rows], c_rs.at[1])
     arrived(wf.at[dp + 1 - 2 * core], w_rs.at[dp + 1 - 2 * core])
     arrived(wf.at[other + 1 - 2 * core], w_rs.at[other + 1 - 2 * core])
-    grad_context = last_last(gl[pl.ds(core * 2, 2)].reshape(256, D), wf[pl.ds(xl * 2, 2)].reshape(HALF, D))
+    projected = first_first(cf[...], wf[...].reshape(HW, D))
+    for block in range(11):
+        cols = slice(block * 128, (block + 1) * 128)
+        att_ref[:, cols] = jnp.where(own_live, projected[:, cols], 0.0).astype(BF)
+    write(att_ref, att_hbm)
+
+    relay_cotangent(ORDER[3])
+    weight_piece(ORDER[3])
+
+    @pl.when(y != 3)
+    def _():
+        extra_copy().start()
+
+    grad_context = None
+    for piece in range(4):
+        width = min(PIECE, D - piece * PIECE)
+        part = last_last(
+            gl[piece, pl.ds(core * 2, 2), :, 0:width].reshape(256, width),
+            wf[pl.ds(xl * 2, 2), :, piece * PIECE:piece * PIECE + width].reshape(HALF, width))
+        grad_context = part if grad_context is None else grad_context + part
     g_buf[...] = grad_context.astype(BF)
     gt_buf[...] = jnp.transpose(grad_context).astype(BF)
 
-    arrived(ct.at[1 - core], c_rs.at[0])
-    for slot in range(2):
-        there = (1 - core) * 2 + slot
-        arrived(gl.at[there], gl_rs.at[there])
-    context = jnp.concatenate([ct[0], ct[1]], axis=1)
-    for start in range(0, D, 256):
-        stop = min(start + 256, D)
-        part = plain(context, gl[:, :, start:stop].reshape(512, stop - start))
-        for column in range(start, stop, 128):
-            for row in range(11):
-                tile = row * 11 + column // 128
-                dw[tile // 32, tile % 32] = part[row * 16:row * 16 + 16, column - start:column - start + 128].astype(BF)
-    for tile in range(TILES, 128):
-        dw[tile // 32, tile % 32] = jnp.zeros((16, 128), BF)
-    for step in (1, 3, 2):
-        goal = lax.rem(y + step, 4)
-        send(dw.at[goal], ry.at[step - 1], y_rs.at[step - 1], (dp, lax.rem(place + 32 * step, PLACES)))
-
-    for head in range(4):
+    for step in range(3):
+        arrived(ry.at[step], y_rs.at[step])
+    total = dw[y].astype(F32) + ry[0].astype(F32) + ry[1].astype(F32) + ry[2].astype(F32)
+    sx[...] = total.astype(BF).reshape(8, 4, 16, 128)
+
+    @pl.when(y == 3)
+    def _():
+        for source in range(3):
+            arrived(ryx.at[source], yx_rs.at[source])
+        for tile in range(22, 25):
+            own = tile - 22
+            total = dwx[own].astype(F32)
+            for source in range(3):
+                total = total + ryx[source, own].astype(F32)
+            sx[tile // 4, tile % 4] = total.astype(BF)
+
+    def stays(half, b):
+        return (xh == xl) & (xl == half) & (inner == b)
+
+    def quad_copy(n):
+        half, b = lax.div(n, 4), lax.rem(n, 4)
+        return pltpu.make_async_remote_copy(
+            src_ref=sx.at[n], dst_ref=rx.at[xh * 4 + inner], send_sem=x_ss.at[n], recv_sem=x_rs.at[xh * 4 + inner],
+            device_id=quad(xl * 2 + half, b), device_id_type=MESH)
+
+    def quad_start(n, carry):
+        @pl.when(jnp.logical_not(stays(lax.div(n, 4), lax.rem(n, 4))))
+        def _():
+            quad_copy(n).start()
+
+        return carry
+
+    def quad_sent(n, carry):
+        @pl.when(jnp.logical_not(stays(lax.div(n, 4), lax.rem(n, 4))))
+        def _():
+            quad_copy(n).wait_send()
+
+        return carry
+
+    def quad_here(n, carry):
+        @pl.when(jnp.logical_not((xh == xl) & (n == xh * 4 + inner)))
+        def _():
+            arrived(rx.at[n], x_rs.at[n])
+
+        return carry
+
+    lax.fori_loop(0, 8, quad_start, 0)
+
+    @pl.when(xh == xl)
+    def _():
+        rx[xh * 4 + inner] = sx[xl * 4 + inner]
+
+    def backward(head):
         low, high = WINDOWS[head]
         g_head = g_buf[:, low:high] * head_mask(head, 256).astype(BF)
         delta = None
@@ -282,66 +379,24 @@
         dk_acc[rows, :] = stripe(head, plain(lanes(qw, first, stop, 0, 2), ds_buf[...])) * SCALE
         dv_acc[rows, :] = stripe(head, plain(gt_buf[first:stop, :], probs[head]))
         dq_acc[rows, :] = stripe(head, last_last(lanes(kw, first, stop, 0, SLOTS), ds_buf[...])) * SCALE
-        if head % 2 == 1:
-            piece = head // 2
-            block = slice(piece * BLOCK, (piece + 1) * BLOCK)
-            for side in range(2):
-                cols = slice(side * 512, side * 512 + 256)
-                kvb[side, piece, 0] = dk_acc[block, cols].astype(BF)
-                kvb[side, piece, 1] = dv_acc[block, cols].astype(BF)
-                send(kvb.at[side, piece], rkv.at[1 - side, piece], kv_rs.at[1 - side, piece], (behind, ahead)[side])
+
+    def send_terms(piece):
+        block = slice(piece * BLOCK, (piece + 1) * BLOCK)
+        for side in range(2):
+            cols = slice(side * 512, side * 512 + 256)
+            kvb[side, piece, 0] = dk_acc[block, cols].astype(BF)
+            kvb[side, piece, 1] = dv_acc[block, cols].astype(BF)
+            send(kvb.at[side, piece], rkv.at[1 - side, piece], kv_rs.at[1 - side, piece], (behind, ahead)[side])
+
+    backward(0)
+    backward(1)
+    send_terms(0)
+    backward(2)
+    backward(3)
     dqw[0] = dq_acc[:, 0:128].astype(BF)
     dqw[1] = dq_acc[:, 128:256].astype(BF)
     send(dqw.at[1 - xl], dqf, dq_rs, partner)
     write(dqw.at[xl], gq_hbm.at[near_rows])
-
-    for step in range(3):
-        arrived(ry.at[step], y_rs.at[step])
-    total = dw[y].astype(F32) + ry[0].astype(F32) + ry[1].astype(F32) + ry[2].astype(F32)
-    sx[...] = total.astype(BF).reshape(8, 4, 16, 128)
-
-    def stays(half, b):
-        return (xh == xl) & (xl == half) & (inner == b)
-
-    def quad_copy(n):
-        half, b = lax.div(n, 4), lax.rem(n, 4)
-        return pltpu.make_async_remote_copy(
-            src_ref=sx.at[n], dst_ref=rx.at[xh * 4 + inner], send_sem=x_ss.at[n], recv_sem=x_rs.at[xh * 4 + inner],
-            device_id=quad(xl * 2 + half, b), device_id_type=MESH)
-
-    def quad_start(n, carry):
-        @pl.when(jnp.logical_not(stays(lax.div(n, 4), lax.rem(n, 4))))
-        def _():
-            quad_copy(n).start()
-
-        return carry
-
-    def quad_sent(n, carry):
-        @pl.when(jnp.logical_not(stays(lax.div(n, 4), lax.rem(n, 4))))
-        def _():
-            quad_copy(n).wait_send()
-
-        return carry
-
-    def quad_here(n, carry):
-        @pl.when(jnp.logical_not((xh == xl) & (n == xh * 4 + inner)))
-        def _():
-            arrived(rx.at[n], x_rs.at[n])
-
-        return carry
-
-    lax.fori_loop(0, 8, quad_start, 0)
-
-    @pl.when(xh == xl)
-    def _():
-        rx[xh * 4 + inner] = sx[xl * 4 + inner]
-
-    arrived(cf.at[away_rows], c_rs.at[1])
-    projected = first_first(cf[...], wf[...].reshape(HW, D))
-    for block in range(11):
-        cols = slice(block * 128, (block + 1) * 128)
-        att_ref[:, cols] = jnp.where(own_live, projected[:, cols], 0.0).astype(BF)
-    write(att_ref, att_hbm)
 
     lax.fori_loop(0, 8, quad_here, 0)
     total = rx[0].astype(F32)
@@ -351,17 +406,23 @@
     for step in (2, 1, 3):
         send(fr.at[group], fr.at[group], f_rs.at[group], far(step))
 
-    for piece in range(2):
+    def sum_terms(piece):
         block = slice(piece * BLOCK, (piece + 1) * BLOCK)
         for side in range(2):
             arrived(rkv.at[side, piece], kv_rs.at[side, piece])
         for which, acc in ((0, dk_acc), (1, dv_acc)):
             value = acc[block, 256:512] + rkv[0, piece, which].astype(F32) + rkv[1, piece, which].astype(F32)
-            kvs[0, which, block, :] = value[:, 0:128].astype(BF)
-            kvs[1, which, block, :] = value[:, 128:256].astype(BF)
-    send(kvs.at[1 - xl], kvf, kvf_rs, partner)
-    write(kvs.at[xl, 0], gk_hbm.at[near_rows])
-    write(kvs.at[xl, 1], gv_hbm.at[near_rows])
+            kvs[0, piece, which] = value[:, 0:128].astype(BF)
+            kvs[1, piece, which] = value[:, 128:256].astype(BF)
+        send(kvs.at[1 - xl, piece], kvf.at[piece], kvf_rs.at[piece], partner)
+        write_terms(kvs.at[xl, piece], xl, piece)
+
+    def write_terms(source, half, piece):
+        rows = pl.ds(pl.multiple_of(half * HALF + piece * BLOCK, 16), BLOCK)
+        write(source.at[0], gk_hbm.at[rows])
+        write(source.at[1], gv_hbm.at[rows])
+
+    sum_terms(0)
     arrived(dqf, dq_rs)
     write(dqf, gq_hbm.at[away_rows])
 
@@ -386,17 +447,23 @@
     three = incoming(gf.at[0, pl.ds(0, 3)], z_rs.at[0], z_ss.at[0])
     seven = incoming(gf.at[pl.ds(0, 7)], z_rs.at[1], z_ss.at[1])
     lax.fori_loop(1, 4, spread, 0)
+    send_terms(1)
     three.wait_recv()
     lax.fori_loop(1, 8, share, 0)
 
-    arrived(kvf, kvf_rs)
-    write(kvf.at[0], gk_hbm.at[away_rows])
-    write(kvf.at[1], gv_hbm.at[away_rows])
+    sum_terms(1)
+    for piece in range(2):
+        arrived(kvf.at[piece], kvf_rs.at[piece])
+        write_terms(kvf.at[piece], 1 - xl, piece)
 
     seven.wait_recv()
     write(gf, gw_hbm)
     for copy in sent:
         copy.wait_send()
+    @pl.when(y != 3)
+    def _():
+        extra_copy().wait_send()
+
     lax.fori_loop(0, 8, quad_sent, 0)
     three.wait_send()
     seven.wait_send()
@@ -419,7 +486,9 @@
         copy.start()
     reads[0].wait()
     for tile in range(TILES):
-        row, column = tile // 11, tile % 11
+        row, column = tile % 32 % 11, tile // 32 * 3 + tile % 32 // 11
+        if tile >= 96 + 22:
+            row, column = 10, (tile - 118) * 3 + 2
         gw[row * 16:row * 16 + 16, column * 128:(column + 1) * 128] = tiles[
             tile // 16, tile // 4 % 4, tile % 4].astype(F32)
     writes[0].start()
@@ -437,7 +506,7 @@
         pltpu.VMEM((PLACES, ROWS), jnp.int32), pltpu.SMEM((1, PLACES), jnp.int32), pltpu.VMEM((ROWS, D), BF),
         pltpu.VMEM((ROWS, D), BF),
         pltpu.VMEM(window, BF), pltpu.VMEM(window, BF), pltpu.VMEM(halves, BF), pltpu.VMEM((256, HALF), BF),
-        pltpu.VMEM((4, ROWS, D), BF), pltpu.VMEM((4, BLOCK, D), BF),
+        pltpu.VMEM((4, 4, ROWS, PIECE), BF), pltpu.VMEM((4, BLOCK, D), BF),
         pltpu.VMEM((256, 768), F32), pltpu.VMEM((256, 768), F32),
         pltpu.VMEM((4, 256, 768), BF), pltpu.VMEM((256, 768), BF),
         pltpu.VMEM((HALF, 256), F32), pltpu.VMEM((HALF, 256), BF), pltpu.VMEM(halves, BF), pltpu.VMEM((HW, ROWS), BF),
@@ -445,13 +514,14 @@
         pltpu.VMEM((HALF, 256), F32), pltpu.VMEM((HALF, 768), F32), pltpu.VMEM((HALF, 768), F32),
         pltpu.VMEM(halves, BF), pltpu.VMEM((HALF, ROWS), BF),
         pltpu.VMEM((2, 2, 2, BLOCK, 256), BF), pltpu.VMEM((2, 2, 2, BLOCK, 256), BF),
-        pltpu.VMEM((2, 2, HALF, ROWS), BF), pltpu.VMEM((2, HALF, ROWS), BF),
-        pltpu.VMEM((4, 32, 16, 128), BF), pltpu.VMEM((3, 32, 16, 128), BF),
+        pltpu.VMEM((2, 2, 2, BLOCK, ROWS), BF), pltpu.VMEM((2, 2, BLOCK, ROWS), BF),
+        pltpu.VMEM((4, 32, 16, 128), BF), pltpu.VMEM((4, 16, 128), BF),
+        pltpu.VMEM((3, 32, 16, 128), BF), pltpu.VMEM((3, 3, 16, 128), BF),
         pltpu.VMEM((8, 4, 16, 128), BF), pltpu.VMEM((8, 4, 16, 128), BF),
         pltpu.VMEM((4, 4, 16, 128), BF), pltpu.VMEM(tiles, BF),
-        dma((6,)), dma((6,)), dma, dma((4,)), dma((4,)), dma((2,)), dma, dma((2, 2)), dma, dma((3,)), dma((8,)),
+        dma((6,)), dma((6,)), dma, dma((4, 4)), dma((4,)), dma((2,)), dma, dma((2, 2)), dma((2,)), dma((3,)), dma((3,)), dma((8,)),
         dma((4,)), dma((2,)),
-        dma((40,)), dma((8,)), dma((2,)), dma((7,)), dma((8,)),
+        dma((40,)), dma, dma((8,)), dma((2,)), dma((7,)), dma((12,)),
     ]
     shapes = (
         jax.ShapeDtypeStruct((ROWS, D), BF),

time: 74.1 us -> 70.1 us (0.946)
  the two profiles are of different devices: /device:TPU:1 before, /device:TPU:6 now
where the time goes in v4:
time: 70.1 us; the launch traced here: 69.9 us
  Pallas kernels  69.3 us (99%)
    pallas_call x1, Pallas kernels, per_device(): pl.pallas_call(kernel, out_shape=shapes + (jax.ShapeDtypeStruct(tiles, BF...  66.8 us
    pallas_call x1, Pallas kernels, per_device(): pl.pallas_call(hand_over, out_shape=shapes + (jax.ShapeDtypeStruct((BLOCK...  2.48 us

profile of v4, /device:TPU:6, one launch (start us, length us, event | category | flops | bytes accessed | tf_op | source)
XLA Modules:
  0.0 69.9 jit_solution(9133899510844452474)
XLA Ops:
  0.6 66.8 %shard_map.110 = (bf16[128,1408]{1,0:T(8,128)(2,1)}, bf16[704,128]{1,0:T(8,128)(2,1)}, bf16[704,128]{1,0:T(8,128)(2,1)}, bf16[704,128]{1,0:T(8,128)(2,1)}, bf16[8,4,4,16,128]{4,3,2,1,0:T(8,128)(2,1)}) custom-call(bf16[704,128]{1,0:T(8,128)(2,1)} %bitcast.23, bf16[704,128]{1,0:T(8,128)(2,1)} %bitcast.24, bf16[704,128]{1,0:T(8,128)(2,1)} %bitcast.25, ...), custom_call_target="tpu_custom_call" | custom-call | flops 1500000000 | bytes 4000000 | tf_op jit(solution)/shard_map/pallas_call | solution.py:532
  67.4 2.5 %shard_map.111 = (bf16[128,1408]{1,0:T(8,128)(2,1)}, bf16[704,128]{1,0:T(8,128)(2,1)}, bf16[704,128]{1,0:T(8,128)(2,1)}, bf16[704,128]{1,0:T(8,128)(2,1)}, f32[176,1408]{1,0:T(8,128)}) custom-call(bf16[128,1408]{1,0:T(8,128)(2,1)} %get-tuple-element.15.att_in, bf16[704,128]{1,0:T(8,128)(2,1)} %get-tuple-element.16.gq_in, ...), custom_call_target="tpu_custom_call" | custom-call | tf_op jit(solution)/shard_map/pallas_call | solution.py:542

commit v5 on v4

--- a/solution.py
+++ b/solution.py
@@ -90,6 +90,39 @@
 
     near_rows = pl.ds(pl.multiple_of(xl * HALF, 16), HALF)
     away_rows = pl.ds(pl.multiple_of((1 - xl) * HALF, 16), HALF)
+    written = []
+
+    def write(source, target):
+        written.append(pltpu.make_async_copy(source, target, out_sems.at[len(written)]))
+        written[-1].start()
+
+    barrier = pltpu.get_barrier_semaphore()
+
+    def greet(device):
+        pl.semaphore_signal(barrier, inc=1, device_id=device, device_id_type=MESH)
+
+    def greet_quad(j, carry):
+        at = lax.rem((xh * 2 + xl) * 4 + inner + j, 16)
+        greet(quad(lax.div(at, 4), lax.rem(at, 4)))
+        return carry
+
+    def greet_around(j, carry):
+        greet(around(j))
+        return carry
+
+    def greet_far(j, carry):
+        greet(far(j))
+        return carry
+
+    for device in (ahead, behind, twin):
+        greet(device)
+    lax.fori_loop(1, 4, greet_far, 0)
+    lax.fori_loop(1, 16, greet_quad, 0)
+    lax.fori_loop(1, 8, greet_around, 0)
+
+    def piece_at(step):
+        return lax.rem(y + step, 4)
+
     fetches = []
     for source, target in (
             (cot_hbm, cot_ref), (cnt_hbm, cnt_ref), (pid_hbm, pid_ref), (k_ref.at[near_rows], kw.at[2 + xl]),
@@ -97,36 +130,33 @@
         fetches.append(pltpu.make_async_copy(source, target, in_sems.at[len(fetches)]))
         fetches[-1].start()
 
-    written = []
-
-    def write(source, target):
-        written.append(pltpu.make_async_copy(source, target, out_sems.at[len(written)]))
-        written[-1].start()
-
-    barrier = pltpu.get_barrier_semaphore()
-
-    def greet(device):
-        pl.semaphore_signal(barrier, inc=1, device_id=device, device_id_type=MESH)
-
-    def greet_quad(j, carry):
-        at = lax.rem((xh * 2 + xl) * 4 + inner + j, 16)
-        greet(quad(lax.div(at, 4), lax.rem(at, 4)))
-        return carry
-
-    def greet_around(j, carry):
-        greet(around(j))
-        return carry
-
-    def greet_far(j, carry):
-        greet(far(j))
-        return carry
-
-    for device in (ahead, behind, twin):
-        greet(device)
-    lax.fori_loop(1, 4, greet_far, 0)
-    lax.fori_loop(1, 16, greet_quad, 0)
-    lax.fori_loop(1, 8, greet_around, 0)
-
+    pl.semaphore_wait(barrier, 28)
+
+    sent = []
+
+    def send(source, target, recv_sem, device):
+        copy = pltpu.make_async_remote_copy(
+            src_ref=source, dst_ref=target, send_sem=ss.at[len(sent)], recv_sem=recv_sem,
+            device_id=device, device_id_type=MESH)
+        copy.start()
+        sent.append(copy)
+
+    def incoming(ref, recv_sem, send_sem):
+        return pltpu.make_async_remote_copy(
+            src_ref=ref, dst_ref=ref, send_sem=send_sem, recv_sem=recv_sem,
+            device_id=partner, device_id_type=MESH)
+
+    def arrived(ref, recv_sem):
+        incoming(ref, recv_sem, ss.at[0]).wait_recv()
+
+    away = 3 - xl
+    send(k_ref.at[away_rows], kw.at[2 + xl], k_rs.at[2 + xl], partner)
+    send(k_ref.at[near_rows], kw.at[xl], k_rs.at[xl], ahead)
+    send(k_ref.at[near_rows], kw.at[4 + xl], k_rs.at[4 + xl], behind)
+    send(v_ref.at[away_rows], vw.at[2 + xl], v_rs.at[2 + xl], partner)
+    send(v_ref.at[near_rows], vw.at[xl], v_rs.at[xl], ahead)
+    send(v_ref.at[near_rows], vw.at[4 + xl], v_rs.at[4 + xl], behind)
+    send(q_ref.at[away_rows], qw.at[xl], q_rs, partner)
     fetches[0].wait()
     fetches[1].wait()
     own_live = lax.broadcasted_iota(jnp.int32, (ROWS, 128), 0) < cnt_ref[0, place]
@@ -137,36 +167,6 @@
         gl[block // 3, mine, :, inside] = jnp.where(own_live, cot_ref[:, cols].astype(F32), 0.0).astype(BF)
     gl[3, mine, :, 256:384] = jnp.zeros((ROWS, 128), BF)
 
-    def piece_at(step):
-        return lax.rem(y + step, 4)
-
-    pl.semaphore_wait(barrier, 28)
-
-    sent = []
-
-    def send(source, target, recv_sem, device):
-        copy = pltpu.make_async_remote_copy(
-            src_ref=source, dst_ref=target, send_sem=ss.at[len(sent)], recv_sem=recv_sem,
-            device_id=device, device_id_type=MESH)
-        copy.start()
-        sent.append(copy)
-
-    def incoming(ref, recv_sem, send_sem):
-        return pltpu.make_async_remote_copy(
-            src_ref=ref, dst_ref=ref, send_sem=send_sem, recv_sem=recv_sem,
-            device_id=partner, device_id_type=MESH)
-
-    def arrived(ref, recv_sem):
-        incoming(ref, recv_sem, ss.at[0]).wait_recv()
-
-    away = 3 - xl
-    send(k_ref.at[away_rows], kw.at[2 + xl], k_rs.at[2 + xl], partner)
-    send(k_ref.at[near_rows], kw.at[xl], k_rs.at[xl], ahead)
-    send(k_ref.at[near_rows], kw.at[4 + xl], k_rs.at[4 + xl], behind)
-    send(v_ref.at[away_rows], vw.at[2 + xl], v_rs.at[2 + xl], partner)
-    send(v_ref.at[near_rows], vw.at[xl], v_rs.at[xl], ahead)
-    send(v_ref.at[near_rows], vw.at[4 + xl], v_rs.at[4 + xl], behind)
-    send(q_ref.at[away_rows], qw.at[xl], q_rs, partner)
     for step in ORDER:
         here = gl.at[piece_at(step), mine]
         send(here, here, gl_rs.at[mine, step], partner)
@@ -248,7 +248,6 @@
     send(cb.at[pl.ds(pl.multiple_of((1 - core) * BLOCK, 16), BLOCK)], ct.at[core], c_rs.at[0], twin)
     cw[0] = cb[:, 0:128]
     cw[1] = cb[:, 128:256]
-    send(cw.at[1 - xl], cf.at[near_rows], c_rs.at[1], partner)
     ct[core] = cb[core_rows, :]
     cf[near_rows, :] = cw[xl]
 
@@ -283,22 +282,16 @@
     relay_cotangent(ORDER[2])
     weight_piece(ORDER[2])
 
-    arrived(cf.at[away_rows], c_rs.at[1])
-    arrived(wf.at[dp + 1 - 2 * core], w_rs.at[dp + 1 - 2 * core])
-    arrived(wf.at[other + 1 - 2 * core], w_rs.at[other + 1 - 2 * core])
-    projected = first_first(cf[...], wf[...].reshape(HW, D))
-    for block in range(11):
-        cols = slice(block * 128, (block + 1) * 128)
-        att_ref[:, cols] = jnp.where(own_live, projected[:, cols], 0.0).astype(BF)
-    write(att_ref, att_hbm)
-
     relay_cotangent(ORDER[3])
+    send(cw.at[1 - xl], cf.at[near_rows], c_rs.at[1], partner)
     weight_piece(ORDER[3])
 
     @pl.when(y != 3)
     def _():
         extra_copy().start()
 
+    arrived(wf.at[dp + 1 - 2 * core], w_rs.at[dp + 1 - 2 * core])
+    arrived(wf.at[other + 1 - 2 * core], w_rs.at[other + 1 - 2 * core])
     grad_context = None
     for piece in range(4):
         width = min(PIECE, D - piece * PIECE)
@@ -398,6 +391,13 @@
     send(dqw.at[1 - xl], dqf, dq_rs, partner)
     write(dqw.at[xl], gq_hbm.at[near_rows])
 
+    arrived(cf.at[away_rows], c_rs.at[1])
+    projected = first_first(cf[...], wf[...].reshape(HW, D))
+    for block in range(11):
+        cols = slice(block * 128, (block + 1) * 128)
+        att_ref[:, cols] = jnp.where(own_live, projected[:, cols], 0.0).astype(BF)
+    write(att_ref, att_hbm)
+
     lax.fori_loop(0, 8, quad_here, 0)
     total = rx[0].astype(F32)
     for source in range(1, 8):
@@ -405,6 +405,7 @@
     fr[group] = total.astype(BF)
     for step in (2, 1, 3):
         send(fr.at[group], fr.at[group], f_rs.at[group], far(step))
+    send_terms(1)
 
     def sum_terms(piece):
         block = slice(piece * BLOCK, (piece + 1) * BLOCK)
@@ -447,7 +448,6 @@
     three = incoming(gf.at[0, pl.ds(0, 3)], z_rs.at[0], z_ss.at[0])
     seven = incoming(gf.at[pl.ds(0, 7)], z_rs.at[1], z_ss.at[1])
     lax.fori_loop(1, 4, spread, 0)
-    send_terms(1)
     three.wait_recv()
     lax.fori_loop(1, 8, share, 0)
 

time: 70.1 us -> 68.2 us (0.973)
  Pallas kernels: 69.3 us -> 67.4 us
    pallas_call x1, Pallas kernels: 66.8 us -> 64.9 us  [per_device(): pl.pallas_call(kernel, out_shape=shapes + (jax.ShapeDtypeStruct(tiles, BF...]
where the time goes in v5:
time: 68.2 us; the launch traced here: 68 us
  Pallas kernels  67.4 us (99%)
    pallas_call x1, Pallas kernels, per_device(): pl.pallas_call(kernel, out_shape=shapes + (jax.ShapeDtypeStruct(tiles, BF...  64.9 us
    pallas_call x1, Pallas kernels, per_device(): pl.pallas_call(hand_over, out_shape=shapes + (jax.ShapeDtypeStruct((BLOCK...  2.48 us

profile of v5, /device:TPU:6, one launch (start us, length us, event | category | flops | bytes accessed | tf_op | source)
XLA Modules:
  0.0 68.0 jit_solution(10425465435872246141)
XLA Ops:
  0.6 64.9 %shard_map.110 = (bf16[128,1408]{1,0:T(8,128)(2,1)}, bf16[704,128]{1,0:T(8,128)(2,1)}, bf16[704,128]{1,0:T(8,128)(2,1)}, bf16[704,128]{1,0:T(8,128)(2,1)}, bf16[8,4,4,16,128]{4,3,2,1,0:T(8,128)(2,1)}) custom-call(bf16[704,128]{1,0:T(8,128)(2,1)} %bitcast.23, bf16[704,128]{1,0:T(8,128)(2,1)} %bitcast.24, bf16[704,128]{1,0:T(8,128)(2,1)} %bitcast.25, ...), custom_call_target="tpu_custom_call" | custom-call | flops 1500000000 | bytes 4000000 | tf_op jit(solution)/shard_map/pallas_call | solution.py:532
  65.6 2.5 %shard_map.111 = (bf16[128,1408]{1,0:T(8,128)(2,1)}, bf16[704,128]{1,0:T(8,128)(2,1)}, bf16[704,128]{1,0:T(8,128)(2,1)}, bf16[704,128]{1,0:T(8,128)(2,1)}, f32[176,1408]{1,0:T(8,128)}) custom-call(bf16[128,1408]{1,0:T(8,128)(2,1)} %get-tuple-element.15.att_in, bf16[704,128]{1,0:T(8,128)(2,1)} %get-tuple-element.16.gq_in, ...), custom_call_target="tpu_custom_call" | custom-call | tf_op jit(solution)/shard_map/pallas_call | solution.py:542

commit v6 on v5

--- a/solution.py
+++ b/solution.py
@@ -55,9 +55,9 @@
            pid_ref, cnt_ref, cot_ref, att_ref,
            kw, vw, qw, qn, gl, wf, bias, s_buf, probs, ds_buf,
            ctx_acc, cb, cw, cf, ct, g_buf, gt_buf, dq_acc, dk_acc, dv_acc, dqw, dqf,
-           kvb, rkv, kvs, kvf,
+           kb, vb, rk, rv, ks, vs, kf, vf,
            dw, dwx, ry, ryx, sx, rx, fr, gf,
-           k_rs, v_rs, q_rs, gl_rs, w_rs, c_rs, dq_rs, kv_rs, kvf_rs, y_rs, yx_rs, x_rs, f_rs, z_rs,
+           k_rs, v_rs, q_rs, gl_rs, w_rs, c_rs, dq_rs, kt_rs, vt_rs, kf_rs, vf_rs, y_rs, yx_rs, x_rs, f_rs, z_rs,
            ss, y_ss, x_ss, z_ss, in_sems, out_sems):
     dp = lax.axis_index("dp")
     place = lax.axis_index("ctx")
@@ -302,6 +302,13 @@
     g_buf[...] = grad_context.astype(BF)
     gt_buf[...] = jnp.transpose(grad_context).astype(BF)
 
+    for head in range(4):
+        first, stop = STRIPES[head]
+        dv_acc[head * HEAD:(head + 1) * HEAD, :] = stripe(head, plain(gt_buf[first:stop, :], probs[head]))
+    for side in range(2):
+        vb[side] = dv_acc[:, side * 512:side * 512 + 256].astype(BF)
+        send(vb.at[side], rv.at[1 - side], vt_rs.at[1 - side], (behind, ahead)[side])
+
     for step in range(3):
         arrived(ry.at[step], y_rs.at[step])
     total = dw[y].astype(F32) + ry[0].astype(F32) + ry[1].astype(F32) + ry[2].astype(F32)
@@ -370,16 +377,14 @@
         rows = slice(head * HEAD, (head + 1) * HEAD)
         first, stop = STRIPES[head]
         dk_acc[rows, :] = stripe(head, plain(lanes(qw, first, stop, 0, 2), ds_buf[...])) * SCALE
-        dv_acc[rows, :] = stripe(head, plain(gt_buf[first:stop, :], probs[head]))
         dq_acc[rows, :] = stripe(head, last_last(lanes(kw, first, stop, 0, SLOTS), ds_buf[...])) * SCALE
 
     def send_terms(piece):
         block = slice(piece * BLOCK, (piece + 1) * BLOCK)
         for side in range(2):
             cols = slice(side * 512, side * 512 + 256)
-            kvb[side, piece, 0] = dk_acc[block, cols].astype(BF)
-            kvb[side, piece, 1] = dv_acc[block, cols].astype(BF)
-            send(kvb.at[side, piece], rkv.at[1 - side, piece], kv_rs.at[1 - side, piece], (behind, ahead)[side])
+            kb[side, piece] = dk_acc[block, cols].astype(BF)
+            send(kb.at[side, piece], rk.at[1 - side, piece], kt_rs.at[1 - side, piece], (behind, ahead)[side])
 
     backward(0)
     backward(1)
@@ -407,23 +412,30 @@
         send(fr.at[group], fr.at[group], f_rs.at[group], far(step))
     send_terms(1)
 
-    def sum_terms(piece):
+    def sum_values():
+        for side in range(2):
+            arrived(rv.at[side], vt_rs.at[side])
+        value = dv_acc[:, 256:512] + rv[0].astype(F32) + rv[1].astype(F32)
+        vs[0] = value[:, 0:128].astype(BF)
+        vs[1] = value[:, 128:256].astype(BF)
+        send(vs.at[1 - xl], vf, vf_rs, partner)
+        write(vs.at[xl], gv_hbm.at[near_rows])
+
+    def key_rows(half, piece):
+        return gk_hbm.at[pl.ds(pl.multiple_of(half * HALF + piece * BLOCK, 16), BLOCK)]
+
+    def sum_keys(piece):
         block = slice(piece * BLOCK, (piece + 1) * BLOCK)
         for side in range(2):
-            arrived(rkv.at[side, piece], kv_rs.at[side, piece])
-        for which, acc in ((0, dk_acc), (1, dv_acc)):
-            value = acc[block, 256:512] + rkv[0, piece, which].astype(F32) + rkv[1, piece, which].astype(F32)
-            kvs[0, piece, which] = value[:, 0:128].astype(BF)
-            kvs[1, piece, which] = value[:, 128:256].astype(BF)
-        send(kvs.at[1 - xl, piece], kvf.at[piece], kvf_rs.at[piece], partner)
-        write_terms(kvs.at[xl, piece], xl, piece)
-
-    def write_terms(source, half, piece):
-        rows = pl.ds(pl.multiple_of(half * HALF + piece * BLOCK, 16), BLOCK)
-        write(source.at[0], gk_hbm.at[rows])
-        write(source.at[1], gv_hbm.at[rows])
-
-    sum_terms(0)
+            arrived(rk.at[side, piece], kt_rs.at[side, piece])
+        value = dk_acc[block, 256:512] + rk[0, piece].astype(F32) + rk[1, piece].astype(F32)
+        ks[0, piece] = value[:, 0:128].astype(BF)
+        ks[1, piece] = value[:, 128:256].astype(BF)
+        send(ks.at[1 - xl, piece], kf.at[piece], kf_rs.at[piece], partner)
+        write(ks.at[xl, piece], key_rows(xl, piece))
+
+    sum_values()
+    sum_keys(0)
     arrived(dqf, dq_rs)
     write(dqf, gq_hbm.at[away_rows])
 
@@ -448,13 +460,15 @@
     three = incoming(gf.at[0, pl.ds(0, 3)], z_rs.at[0], z_ss.at[0])
     seven = incoming(gf.at[pl.ds(0, 7)], z_rs.at[1], z_ss.at[1])
     lax.fori_loop(1, 4, spread, 0)
+    sum_keys(1)
     three.wait_recv()
     lax.fori_loop(1, 8, share, 0)
 
-    sum_terms(1)
+    arrived(vf, vf_rs)
+    write(vf, gv_hbm.at[away_rows])
     for piece in range(2):
-        arrived(kvf.at[piece], kvf_rs.at[piece])
-        write_terms(kvf.at[piece], 1 - xl, piece)
+        arrived(kf.at[piece], kf_rs.at[piece])
+        write(kf.at[piece], key_rows(1 - xl, piece))
 
     seven.wait_recv()
     write(gf, gw_hbm)
@@ -513,15 +527,18 @@
         pltpu.VMEM((2, BLOCK, 256), BF), pltpu.VMEM((256, HALF), BF), pltpu.VMEM((HALF, 256), BF),
         pltpu.VMEM((HALF, 256), F32), pltpu.VMEM((HALF, 768), F32), pltpu.VMEM((HALF, 768), F32),
         pltpu.VMEM(halves, BF), pltpu.VMEM((HALF, ROWS), BF),
-        pltpu.VMEM((2, 2, 2, BLOCK, 256), BF), pltpu.VMEM((2, 2, 2, BLOCK, 256), BF),
-        pltpu.VMEM((2, 2, 2, BLOCK, ROWS), BF), pltpu.VMEM((2, 2, BLOCK, ROWS), BF),
+        pltpu.VMEM((2, 2, BLOCK, 256), BF), pltpu.VMEM((2, HALF, 256), BF),
+        pltpu.VMEM((2, 2, BLOCK, 256), BF), pltpu.VMEM((2, HALF, 256), BF),
+        pltpu.VMEM((2, 2, BLOCK, ROWS), BF), pltpu.VMEM(halves, BF),
+        pltpu.VMEM((2, BLOCK, ROWS), BF), pltpu.VMEM((HALF, ROWS), BF),
         pltpu.VMEM((4, 32, 16, 128), BF), pltpu.VMEM((4, 16, 128), BF),
         pltpu.VMEM((3, 32, 16, 128), BF), pltpu.VMEM((3, 3, 16, 128), BF),
         pltpu.VMEM((8, 4, 16, 128), BF), pltpu.VMEM((8, 4, 16, 128), BF),
         pltpu.VMEM((4, 4, 16, 128), BF), pltpu.VMEM(tiles, BF),
-        dma((6,)), dma((6,)), dma, dma((4, 4)), dma((4,)), dma((2,)), dma, dma((2, 2)), dma((2,)), dma((3,)), dma((3,)), dma((8,)),
+        dma((6,)), dma((6,)), dma, dma((4, 4)), dma((4,)), dma((2,)), dma, dma((2, 2)), dma((2,)), dma((2,)), dma,
+        dma((3,)), dma((3,)), dma((8,)),
         dma((4,)), dma((2,)),
-        dma((40,)), dma, dma((8,)), dma((2,)), dma((7,)), dma((12,)),
+        dma((48,)), dma, dma((8,)), dma((2,)), dma((7,)), dma((12,)),
     ]
     shapes = (
         jax.ShapeDtypeStruct((ROWS, D), BF),

time: 68.2 us -> 67.2 us (0.985); the launches traced: 68 us -> 66.1 us
  Pallas kernels: 67.4 us -> 65.4 us
    pallas_call x1, Pallas kernels: 64.9 us -> 63 us  [per_device(): pl.pallas_call(kernel, out_shape=shapes + (jax.ShapeDtypeStruct(tiles, BF...]
where the time goes in v6:
time: 67.2 us; the launch traced here: 66.1 us
  Pallas kernels  65.4 us (97%)
    pallas_call x1, Pallas kernels, per_device(): pl.pallas_call(kernel, out_shape=shapes + (jax.ShapeDtypeStruct(tiles, BF...  63 us
    pallas_call x1, Pallas kernels, per_device(): pl.pallas_call(hand_over, out_shape=shapes + (jax.ShapeDtypeStruct((BLOCK...  2.48 us

profile of v6, /device:TPU:6, one launch (start us, length us, event | category | flops | bytes accessed | tf_op | source)
XLA Modules:
  0.0 66.1 jit_solution(4428234615576352714)
XLA Ops:
  0.6 63.0 %shard_map.110 = (bf16[128,1408]{1,0:T(8,128)(2,1)}, bf16[704,128]{1,0:T(8,128)(2,1)}, bf16[704,128]{1,0:T(8,128)(2,1)}, bf16[704,128]{1,0:T(8,128)(2,1)}, bf16[8,4,4,16,128]{4,3,2,1,0:T(8,128)(2,1)}) custom-call(bf16[704,128]{1,0:T(8,128)(2,1)} %bitcast.23, bf16[704,128]{1,0:T(8,128)(2,1)} %bitcast.24, bf16[704,128]{1,0:T(8,128)(2,1)} %bitcast.25, ...), custom_call_target="tpu_custom_call" | custom-call | flops 1500000000 | bytes 4000000 | tf_op jit(solution)/shard_map/pallas_call | solution.py:549
  63.6 2.5 %shard_map.111 = (bf16[128,1408]{1,0:T(8,128)(2,1)}, bf16[704,128]{1,0:T(8,128)(2,1)}, bf16[704,128]{1,0:T(8,128)(2,1)}, bf16[704,128]{1,0:T(8,128)(2,1)}, f32[176,1408]{1,0:T(8,128)}) custom-call(bf16[128,1408]{1,0:T(8,128)(2,1)} %get-tuple-element.15.att_in, bf16[704,128]{1,0:T(8,128)(2,1)} %get-tuple-element.16.gq_in, ...), custom_call_target="tpu_custom_call" | custom-call | tf_op jit(solution)/shard_map/pallas_call | solution.py:559

commit v7 on v6

--- a/solution.py
+++ b/solution.py
@@ -488,24 +488,30 @@
 def hand_over(att_in, gq_in, gk_in, gv_in, gw_in, att_out, gq_out, gk_out, gv_out, gw_out,
               att, gq, gk, gv, tiles, gw, in_sems, out_sems):
     held = (tiles, att, gq, gk, gv)
-    outs = (gw_out, att_out, gq_out, gk_out, gv_out)
     reads = [pltpu.make_async_copy(source, target, in_sems.at[i])
              for i, (source, target) in enumerate(zip((gw_in, att_in, gq_in, gk_in, gv_in), held))]
-    writes = [pltpu.make_async_copy(source, target, out_sems.at[i])
-              for i, (source, target) in enumerate(zip((gw,) + held[1:], outs))]
     for read in reads:
         read.start()
-    for read, copy in list(zip(reads, writes))[1:]:
+    writes = []
+
+    def write(source, target):
+        writes.append(pltpu.make_async_copy(source, target, out_sems.at[len(writes)]))
+        writes[-1].start()
+
+    reads[0].wait()
+    for first, stop in ((0, 6), (6, 11)):
+        for tile in range(TILES):
+            row, column = tile % 32 % 11, tile // 32 * 3 + tile % 32 // 11
+            if tile >= 96 + 22:
+                row, column = 10, (tile - 118) * 3 + 2
+            if first <= row < stop:
+                gw[row * 16:row * 16 + 16, column * 128:(column + 1) * 128] = tiles[
+                    tile // 16, tile // 4 % 4, tile % 4].astype(F32)
+        rows = pl.ds(first * 16, (stop - first) * 16)
+        write(gw.at[rows], gw_out.at[rows])
+    for read, source, target in zip(reads[1:], held[1:], (att_out, gq_out, gk_out, gv_out)):
         read.wait()
-        copy.start()
-    reads[0].wait()
-    for tile in range(TILES):
-        row, column = tile % 32 % 11, tile // 32 * 3 + tile % 32 // 11
-        if tile >= 96 + 22:
-            row, column = 10, (tile - 118) * 3 + 2
-        gw[row * 16:row * 16 + 16, column * 128:(column + 1) * 128] = tiles[
-            tile // 16, tile // 4 % 4, tile % 4].astype(F32)
-    writes[0].start()
+        write(source, target)
     for copy in writes:
         copy.wait()
 
@@ -563,7 +569,7 @@
         out_specs=(hbm,) * 5,
         scratch_shapes=[
             pltpu.VMEM((ROWS, D), BF), pltpu.VMEM((HW, ROWS), BF), pltpu.VMEM((HW, ROWS), BF), pltpu.VMEM((HW, ROWS), BF),
-            pltpu.VMEM(tiles, BF), pltpu.VMEM((BLOCK, D), F32), dma((5,)), dma((5,))],
+            pltpu.VMEM(tiles, BF), pltpu.VMEM((BLOCK, D), F32), dma((5,)), dma((6,))],
         compiler_params=pltpu.CompilerParams(vmem_limit_bytes=VMEM_LIMIT),
     )(*outs)
     attended, grad_queries, grad_keys, grad_values, grad_weight = outs

time: 67.2 us -> 67.2 us (level)
  no operation moved by 1% of the time
where the time goes in v7:
time: 67.2 us; the launch traced here: 66 us
  Pallas kernels  65.4 us (97%)
    pallas_call x1, Pallas kernels, per_device(): pl.pallas_call(kernel, out_shape=shapes + (jax.ShapeDtypeStruct(tiles, BF...  63 us
    pallas_call x1, Pallas kernels, per_device(): pl.pallas_call(hand_over, out_shape=shapes + (jax.ShapeDtypeStruct((BLOCK...  2.41 us

profile of v7, /device:TPU:6, one launch (start us, length us, event | category | flops | bytes accessed | tf_op | source)
XLA Modules:
  0.0 66.0 jit_solution(2910760379053723863)
XLA Ops:
  0.6 63.0 %shard_map.110 = (bf16[128,1408]{1,0:T(8,128)(2,1)}, bf16[704,128]{1,0:T(8,128)(2,1)}, bf16[704,128]{1,0:T(8,128)(2,1)}, bf16[704,128]{1,0:T(8,128)(2,1)}, bf16[8,4,4,16,128]{4,3,2,1,0:T(8,128)(2,1)}) custom-call(bf16[704,128]{1,0:T(8,128)(2,1)} %bitcast.23, bf16[704,128]{1,0:T(8,128)(2,1)} %bitcast.24, bf16[704,128]{1,0:T(8,128)(2,1)} %bitcast.25, ...), custom_call_target="tpu_custom_call" | custom-call | flops 1500000000 | bytes 4000000 | tf_op jit(solution)/shard_map/pallas_call | solution.py:555
  63.6 2.4 %shard_map.111 = (bf16[128,1408]{1,0:T(8,128)(2,1)}, bf16[704,128]{1,0:T(8,128)(2,1)}, bf16[704,128]{1,0:T(8,128)(2,1)}, bf16[704,128]{1,0:T(8,128)(2,1)}, f32[176,1408]{1,0:T(8,128)}) custom-call(bf16[128,1408]{1,0:T(8,128)(2,1)} %get-tuple-element.15.att_in, bf16[704,128]{1,0:T(8,128)(2,1)} %get-tuple-element.16.gq_in, ...), custom_call_target="tpu_custom_call" | custom-call | tf_op jit(solution)/shard_map/pallas_call | solution.py:565

commit v8 on v6

--- a/solution.py
+++ b/solution.py
@@ -114,11 +114,11 @@
         greet(far(j))
         return carry
 
+    lax.fori_loop(1, 4, greet_far, 0)
     for device in (ahead, behind, twin):
         greet(device)
-    lax.fori_loop(1, 4, greet_far, 0)
     lax.fori_loop(1, 16, greet_quad, 0)
-    lax.fori_loop(1, 8, greet_around, 0)
+    lax.fori_loop(2 - xl, 8 - xl, greet_around, 0)
 
     def piece_at(step):
         return lax.rem(y + step, 4)
@@ -130,7 +130,7 @@
         fetches.append(pltpu.make_async_copy(source, target, in_sems.at[len(fetches)]))
         fetches[-1].start()
 
-    pl.semaphore_wait(barrier, 28)
+    pl.semaphore_wait(barrier, 27)
 
     sent = []
 

time: 67.2 us -> 67.2 us (level)
  no operation moved by 1% of the time
where the time goes in v8:
time: 67.2 us; the launch traced here: 66.2 us
  Pallas kernels  65.5 us (97%)
    pallas_call x1, Pallas kernels, per_device(): pl.pallas_call(kernel, out_shape=shapes + (jax.ShapeDtypeStruct(tiles, BF...  63 us
    pallas_call x1, Pallas kernels, per_device(): pl.pallas_call(hand_over, out_shape=shapes + (jax.ShapeDtypeStruct((BLOCK...  2.48 us

profile of v8, /device:TPU:6, one launch (start us, length us, event | category | flops | bytes accessed | tf_op | source)
XLA Modules:
  0.0 66.2 jit_solution(1974125557784545475)
XLA Ops:
  0.6 63.0 %shard_map.110 = (bf16[128,1408]{1,0:T(8,128)(2,1)}, bf16[704,128]{1,0:T(8,128)(2,1)}, bf16[704,128]{1,0:T(8,128)(2,1)}, bf16[704,128]{1,0:T(8,128)(2,1)}, bf16[8,4,4,16,128]{4,3,2,1,0:T(8,128)(2,1)}) custom-call(bf16[704,128]{1,0:T(8,128)(2,1)} %bitcast.23, bf16[704,128]{1,0:T(8,128)(2,1)} %bitcast.24, bf16[704,128]{1,0:T(8,128)(2,1)} %bitcast.25, ...), custom_call_target="tpu_custom_call" | custom-call | flops 1500000000 | bytes 4000000 | tf_op jit(solution)/shard_map/pallas_call | solution.py:549
  63.7 2.5 %shard_map.111 = (bf16[128,1408]{1,0:T(8,128)(2,1)}, bf16[704,128]{1,0:T(8,128)(2,1)}, bf16[704,128]{1,0:T(8,128)(2,1)}, bf16[704,128]{1,0:T(8,128)(2,1)}, f32[176,1408]{1,0:T(8,128)}) custom-call(bf16[128,1408]{1,0:T(8,128)(2,1)} %get-tuple-element.15.att_in, bf16[704,128]{1,0:T(8,128)(2,1)} %get-tuple-element.16.gq_in, ...), custom_call_target="tpu_custom_call" | custom-call | tf_op jit(solution)/shard_map/pallas_call | solution.py:559
